TPU v7x, 32 devices: a whole 2x2x4 slice. The times are simulated.
32 devices in a mesh: dp: 4 (over y, x), fsdp: 8 (over z, core).
Axes of the slice: x: 2, y: 2, z: 4, core: 2. Of those that a mesh axis runs over, the one named last changes fastest.
Arguments:
- inputs: bfloat16 [2, 64, 512, 512], P(None, ('dp', 'fsdp')), may hold values from -6 to 6
- lengths: int32 [2, 64], P(None, ('dp', 'fsdp')), may hold values from 64 to 512, as said below
- grad_out: bfloat16 [2, 64, 512, 512], P(None, ('dp', 'fsdp')), may hold values from -6 to 6
- query_weight: bfloat16 [512, 512], P(('dp', 'fsdp')), may hold values from -0.25 to 0.25
- key_weight: bfloat16 [512, 512], P(('dp', 'fsdp')), may hold values from -0.25 to 0.25
- value_weight: bfloat16 [512, 512], P(('dp', 'fsdp')), may hold values from -0.25 to 0.25
- mix_weight: bfloat16 [512, 512], P(('dp', 'fsdp')), may hold values from -1 to 1
- expand_weight: bfloat16 [512, 2048], P(('dp', 'fsdp')), may hold values from -0.25 to 0.25
- shrink_weight: bfloat16 [2048, 512], P(('dp', 'fsdp')), may hold values from -0.125 to 0.125
- position_table: bfloat16 [512, 512], P(None, ('dp', 'fsdp')), may hold values from -4 to 4
- query_bias: bfloat16 [512], P(('dp', 'fsdp')), may hold values from -3 to 3
- value_bias: bfloat16 [512], P(('dp', 'fsdp')), may hold values from -3 to 3
- mix_bias: bfloat16 [512], P(('dp', 'fsdp')), may hold values from -3 to 3
- expand_bias: bfloat16 [2048], P(('dp', 'fsdp')), may hold values from -3 to 3
- shrink_bias: bfloat16 [512], P(('dp', 'fsdp')), may hold values from -3 to 3
- gain_one: bfloat16 [512], P(('dp', 'fsdp')), may hold values from 0.25 to 1.75
- shift_one: bfloat16 [512], P(('dp', 'fsdp')), may hold values from -3 to 3
- gain_two: bfloat16 [512], P(('dp', 'fsdp')), may hold values from 0.25 to 1.75
- shift_two: bfloat16 [512], P(('dp', 'fsdp')), may hold values from -3 to 3
Outputs:
- output: bfloat16 [2, 64, 512, 512], P(None, ('dp', 'fsdp'))
- grad_inputs: bfloat16 [2, 64, 512, 512], P(None, ('dp', 'fsdp'))
- grad_query_weight: float32 [512, 512], P(('dp', 'fsdp'))
- grad_key_weight: float32 [512, 512], P(('dp', 'fsdp'))
- grad_value_weight: float32 [512, 512], P(('dp', 'fsdp'))
- grad_mix_weight: float32 [512, 512], P(('dp', 'fsdp'))
- grad_expand_weight: float32 [512, 2048], P(('dp', 'fsdp'))
- grad_shrink_weight: float32 [2048, 512], P(('dp', 'fsdp'))
- grad_position_table: float32 [512, 512], P(None, ('dp', 'fsdp'))
- grad_query_bias: float32 [512], P(('dp', 'fsdp'))
- grad_value_bias: float32 [512], P(('dp', 'fsdp'))
- grad_mix_bias: float32 [512], P(('dp', 'fsdp'))
- grad_expand_bias: float32 [2048], P(('dp', 'fsdp'))
- grad_shrink_bias: float32 [512], P(('dp', 'fsdp'))
- grad_gain_one: float32 [512], P(('dp', 'fsdp'))
- grad_shift_one: float32 [512], P(('dp', 'fsdp'))
- grad_gain_two: float32 [512], P(('dp', 'fsdp'))
- grad_shift_two: float32 [512], P(('dp', 'fsdp'))
Inputs may be any that keep to these rules, and one draw needn't show every extreme that they name: `lengths`: number of real characters of each window; the rest of the window is padding. In every draw some window has exactly 512.
All inputs are finite; a program needn't handle non-finite values.
Results may differ from a plain program's by a relative error of at most 0.013.
The roundings to bfloat16 on the way count: a program that leaves them out, or rounds other values in their place, can miss the bound.
Values may be sent and summed in bfloat16 or wider, within the bound.
A program may use at most 192 MiB of HBM per device.

v0:
```python
import jax
import jax.numpy as jnp
from jax import lax
from jax.sharding import PartitionSpec as P

HEADS = 8


epsilon = 1e-05


def norm_apply(summed, gain_vec, shift_vec):
    center = summed - jnp.mean(summed, -1, keepdims=True)
    spread = jnp.mean(center * center, -1, keepdims=True)
    return center * lax.rsqrt(spread + epsilon) * gain_vec + shift_vec


def project(operand, weight):
    return jnp.einsum("wsd,de->wse", operand, weight, preferred_element_type=jnp.float32)


def project_back(gradient, weight):
    return jnp.einsum("wse,de->wsd", gradient, weight, preferred_element_type=jnp.float32)


def weight_grad(operand, gradient):
    return jnp.einsum("wsd,wse->de", operand, gradient, preferred_element_type=jnp.float32)


def row_sum(gradient):
    return jnp.sum(gradient.astype(jnp.float32), axis=(0, 1))


def valid_pairs(window_lengths, seqlen):
    row_ids = lax.broadcasted_iota(jnp.int32, (seqlen, seqlen), 0)
    col_ids = lax.broadcasted_iota(jnp.int32, (seqlen, seqlen), 1)
    return (col_ids <= row_ids)[None, None] & (
        col_ids[None, None] < window_lengths[:, None, None, None]
    )


def scores_of(query_heads, key_heads, allowed, score_scale):
    raw_scores = (
        jnp.einsum("wqhe,wkhe->whqk", query_heads, key_heads, preferred_element_type=jnp.float32)
        * score_scale
    )
    return jnp.where(allowed, raw_scores, -1e30)


def forward_pass(params, window_inputs, window_lengths):
    (
        query_weight,
        key_weight,
        value_weight,
        mix_weight,
        expand_weight,
        shrink_weight,
        position_table,
        query_bias,
        value_bias,
        mix_bias,
        expand_bias,
        shrink_bias,
        gain_one,
        shift_one,
        gain_two,
        shift_two,
    ) = params
    window_count, seqlen, model_width = window_inputs.shape
    head_size = model_width // HEADS
    score_scale = head_size ** (-0.5)
    hidden = window_inputs.astype(jnp.float32) + position_table.astype(jnp.float32)[None]
    hidden_low = hidden.astype(jnp.bfloat16)
    queries = (project(hidden_low, query_weight) + query_bias.astype(jnp.float32)).astype(
        jnp.bfloat16
    )
    keys_low = project(hidden_low, key_weight).astype(jnp.bfloat16)
    values_low = (project(hidden_low, value_weight) + value_bias.astype(jnp.float32)).astype(
        jnp.bfloat16
    )
    query_heads = queries.reshape(window_count, seqlen, HEADS, head_size)
    key_heads = keys_low.reshape(window_count, seqlen, HEADS, head_size)
    value_heads = values_low.reshape(window_count, seqlen, HEADS, head_size)
    allowed = valid_pairs(window_lengths, seqlen)
    masked = scores_of(query_heads, key_heads, allowed, score_scale)
    row_top = jnp.max(masked, -1, keepdims=True)
    exponent = jnp.exp(masked - row_top)
    denom_sum = jnp.sum(exponent, -1, keepdims=True)
    probs_low = (exponent / denom_sum).astype(jnp.bfloat16)
    log_total = row_top + jnp.log(denom_sum)
    mixed_low = jnp.einsum(
        "whqk,wkhe->wqhe", probs_low, value_heads, preferred_element_type=jnp.float32
    )
    mixed_low = mixed_low.astype(jnp.bfloat16).reshape(window_count, seqlen, model_width)
    first_sum = hidden + (project(mixed_low, mix_weight) + mix_bias.astype(jnp.float32))
    normed, norm_first = jax.vjp(
        norm_apply, first_sum, gain_one.astype(jnp.float32), shift_one.astype(jnp.float32)
    )
    normed_low = normed.astype(jnp.bfloat16)
    pre_act = project(normed_low, expand_weight) + expand_bias.astype(jnp.float32)
    activated, gelu_back = jax.vjp(jax.nn.gelu, pre_act)
    act_low = activated.astype(jnp.bfloat16)
    second_sum = normed + (project(act_low, shrink_weight) + shrink_bias.astype(jnp.float32))
    result, norm_second = jax.vjp(
        norm_apply, second_sum, gain_two.astype(jnp.float32), shift_two.astype(jnp.float32)
    )
    saved_state = (
        hidden_low,
        query_heads,
        key_heads,
        value_heads,
        log_total,
        allowed,
        mixed_low,
        norm_first,
        normed_low,
        gelu_back,
        act_low,
        norm_second,
    )
    return (result.astype(jnp.bfloat16), saved_state)


def backward_pass(params, saved_state, cotangent):
    query_weight, key_weight, value_weight, mix_weight, expand_weight, shrink_weight = params[:6]
    (
        hidden_low,
        query_heads,
        key_heads,
        value_heads,
        log_total,
        allowed,
        mixed_low,
        norm_first,
        normed_low,
        gelu_back,
        act_low,
        norm_second,
    ) = saved_state
    window_count, seqlen, model_width = hidden_low.shape
    head_size = model_width // HEADS
    score_scale = head_size ** (-0.5)
    d_second, grad_gain_two, grad_shift_two = norm_second(cotangent)
    grad_ff = d_second.astype(jnp.bfloat16)
    grad_shrink_bias = row_sum(grad_ff)
    grad_shrink = weight_grad(act_low, grad_ff)
    (grad_pre,) = gelu_back(project_back(grad_ff, shrink_weight))
    grad_pre = grad_pre.astype(jnp.bfloat16)
    grad_expand_bias = row_sum(grad_pre)
    grad_expand = weight_grad(normed_low, grad_pre)
    d_normed = d_second + project_back(grad_pre, expand_weight)
    d_first, grad_gain_one, grad_shift_one = norm_first(d_normed)
    grad_attn = d_first.astype(jnp.bfloat16)
    grad_mix_bias = row_sum(grad_attn)
    grad_mix = weight_grad(mixed_low, grad_attn)
    grad_mixed = project_back(grad_attn, mix_weight).astype(jnp.bfloat16)
    grad_mixed = grad_mixed.reshape(window_count, seqlen, HEADS, head_size)
    attn_probs = jnp.exp(scores_of(query_heads, key_heads, allowed, score_scale) - log_total)
    d_probs = jnp.einsum(
        "wqhe,wkhe->whqk", grad_mixed, value_heads, preferred_element_type=jnp.float32
    )
    grad_scores = attn_probs * (d_probs - jnp.sum(attn_probs * d_probs, -1, keepdims=True))
    grad_scores = grad_scores.astype(jnp.bfloat16)
    grad_queries = (
        jnp.einsum("whqk,wkhe->wqhe", grad_scores, key_heads, preferred_element_type=jnp.float32)
        * score_scale
    )
    grad_queries = grad_queries.astype(jnp.bfloat16).reshape(window_count, seqlen, model_width)
    grad_keys = (
        jnp.einsum("whqk,wqhe->wkhe", grad_scores, query_heads, preferred_element_type=jnp.float32)
        * score_scale
    )
    grad_keys = grad_keys.astype(jnp.bfloat16).reshape(window_count, seqlen, model_width)
    grad_values = jnp.einsum(
        "whqk,wqhe->wkhe",
        attn_probs.astype(jnp.bfloat16),
        grad_mixed,
        preferred_element_type=jnp.float32,
    )
    grad_values = grad_values.astype(jnp.bfloat16).reshape(window_count, seqlen, model_width)
    grad_query = weight_grad(hidden_low, grad_queries)
    grad_key = weight_grad(hidden_low, grad_keys)
    grad_value = weight_grad(hidden_low, grad_values)
    grad_query_bias = row_sum(grad_queries)
    grad_value_bias = row_sum(grad_values)
    d_hidden = (
        d_first + project_back(grad_queries, query_weight) + project_back(grad_keys, key_weight)
    )
    d_hidden = d_hidden + project_back(grad_values, value_weight)
    grad_positions = jnp.sum(d_hidden, 0)
    grads = (
        grad_query,
        grad_key,
        grad_value,
        grad_mix,
        grad_expand,
        grad_shrink,
        grad_positions,
        grad_query_bias,
        grad_value_bias,
        grad_mix_bias,
        grad_expand_bias,
        grad_shrink_bias,
        grad_gain_one,
        grad_shift_one,
        grad_gain_two,
        grad_shift_two,
    )
    return (d_hidden.astype(jnp.bfloat16), grads)


def local(
    inputs,
    lengths,
    grad_out,
    query_weight,
    key_weight,
    value_weight,
    mix_weight,
    expand_weight,
    shrink_weight,
    position_table,
    query_bias,
    value_bias,
    mix_bias,
    expand_bias,
    shrink_bias,
    gain_one,
    shift_one,
    gain_two,
    shift_two,
):
    micro_count = inputs.shape[0]
    seqlen = inputs.shape[2]
    accumulated = None
    shard_total = None
    outputs_list = []
    grads_list = []
    for micro_idx in range(micro_count):
        gathered = (
            lax.all_gather(query_weight, ("dp", "fsdp"), axis=0, tiled=True),
            lax.all_gather(key_weight, ("dp", "fsdp"), axis=0, tiled=True),
            lax.all_gather(value_weight, ("dp", "fsdp"), axis=0, tiled=True),
            lax.all_gather(mix_weight, ("dp", "fsdp"), axis=0, tiled=True),
            lax.all_gather(expand_weight, ("dp", "fsdp"), axis=0, tiled=True),
            lax.all_gather(shrink_weight, ("dp", "fsdp"), axis=0, tiled=True),
            lax.all_gather(position_table, ("dp", "fsdp"), axis=1, tiled=True),
            lax.all_gather(query_bias, ("dp", "fsdp"), axis=0, tiled=True),
            lax.all_gather(value_bias, ("dp", "fsdp"), axis=0, tiled=True),
            lax.all_gather(mix_bias, ("dp", "fsdp"), axis=0, tiled=True),
            lax.all_gather(expand_bias, ("dp", "fsdp"), axis=0, tiled=True),
            lax.all_gather(shrink_bias, ("dp", "fsdp"), axis=0, tiled=True),
            lax.all_gather(gain_one, ("dp", "fsdp"), axis=0, tiled=True),
            lax.all_gather(shift_one, ("dp", "fsdp"), axis=0, tiled=True),
            lax.all_gather(gain_two, ("dp", "fsdp"), axis=0, tiled=True),
            lax.all_gather(shift_two, ("dp", "fsdp"), axis=0, tiled=True),
        )
        window_lengths = lengths[micro_idx]
        result, saved_state = forward_pass(gathered, inputs[micro_idx], window_lengths)
        outputs_list.append(result)
        row_ids = lax.broadcasted_iota(jnp.int32, (window_lengths.shape[0], seqlen), 1)
        row_keep = (row_ids < window_lengths[:, None]).astype(jnp.float32)
        cotangent = grad_out[micro_idx].astype(jnp.float32) * row_keep[..., None]
        gathered = (
            lax.all_gather(query_weight, ("dp", "fsdp"), axis=0, tiled=True),
            lax.all_gather(key_weight, ("dp", "fsdp"), axis=0, tiled=True),
            lax.all_gather(value_weight, ("dp", "fsdp"), axis=0, tiled=True),
            lax.all_gather(mix_weight, ("dp", "fsdp"), axis=0, tiled=True),
            lax.all_gather(expand_weight, ("dp", "fsdp"), axis=0, tiled=True),
            lax.all_gather(shrink_weight, ("dp", "fsdp"), axis=0, tiled=True),
            lax.all_gather(position_table, ("dp", "fsdp"), axis=1, tiled=True),
            lax.all_gather(query_bias, ("dp", "fsdp"), axis=0, tiled=True),
            lax.all_gather(value_bias, ("dp", "fsdp"), axis=0, tiled=True),
            lax.all_gather(mix_bias, ("dp", "fsdp"), axis=0, tiled=True),
            lax.all_gather(expand_bias, ("dp", "fsdp"), axis=0, tiled=True),
            lax.all_gather(shrink_bias, ("dp", "fsdp"), axis=0, tiled=True),
            lax.all_gather(gain_one, ("dp", "fsdp"), axis=0, tiled=True),
            lax.all_gather(shift_one, ("dp", "fsdp"), axis=0, tiled=True),
            lax.all_gather(gain_two, ("dp", "fsdp"), axis=0, tiled=True),
            lax.all_gather(shift_two, ("dp", "fsdp"), axis=0, tiled=True),
        )
        grad_acts, grads = backward_pass(gathered, saved_state, cotangent)
        grads_list.append(grad_acts)
        accumulated = (
            grads
            if accumulated is None
            else tuple((first + second for first, second in zip(accumulated, grads)))
        )
    shard_total = (
        lax.psum_scatter(accumulated[0], ("dp", "fsdp"), scatter_dimension=0, tiled=True),
        lax.psum_scatter(accumulated[1], ("dp", "fsdp"), scatter_dimension=0, tiled=True),
        lax.psum_scatter(accumulated[2], ("dp", "fsdp"), scatter_dimension=0, tiled=True),
        lax.psum_scatter(accumulated[3], ("dp", "fsdp"), scatter_dimension=0, tiled=True),
        lax.psum_scatter(accumulated[4], ("dp", "fsdp"), scatter_dimension=0, tiled=True),
        lax.psum_scatter(accumulated[5], ("dp", "fsdp"), scatter_dimension=0, tiled=True),
        lax.psum_scatter(accumulated[6], ("dp", "fsdp"), scatter_dimension=1, tiled=True),
        lax.psum_scatter(accumulated[7], ("dp", "fsdp"), scatter_dimension=0, tiled=True),
        lax.psum_scatter(accumulated[8], ("dp", "fsdp"), scatter_dimension=0, tiled=True),
        lax.psum_scatter(accumulated[9], ("dp", "fsdp"), scatter_dimension=0, tiled=True),
        lax.psum_scatter(accumulated[10], ("dp", "fsdp"), scatter_dimension=0, tiled=True),
        lax.psum_scatter(accumulated[11], ("dp", "fsdp"), scatter_dimension=0, tiled=True),
        lax.psum_scatter(accumulated[12], ("dp", "fsdp"), scatter_dimension=0, tiled=True),
        lax.psum_scatter(accumulated[13], ("dp", "fsdp"), scatter_dimension=0, tiled=True),
        lax.psum_scatter(accumulated[14], ("dp", "fsdp"), scatter_dimension=0, tiled=True),
        lax.psum_scatter(accumulated[15], ("dp", "fsdp"), scatter_dimension=0, tiled=True),
    )
    output = jnp.stack(outputs_list, 0)
    grad_inputs = jnp.stack(grads_list, 0)
    return (
        output,
        grad_inputs,
        shard_total[0],
        shard_total[1],
        shard_total[2],
        shard_total[3],
        shard_total[4],
        shard_total[5],
        shard_total[6],
        shard_total[7],
        shard_total[8],
        shard_total[9],
        shard_total[10],
        shard_total[11],
        shard_total[12],
        shard_total[13],
        shard_total[14],
        shard_total[15],
    )


def solution(mesh):
    placed = (
        P(None, ("dp", "fsdp"), None, None),
        P(None, ("dp", "fsdp")),
        P(None, ("dp", "fsdp"), None, None),
        P(("dp", "fsdp"), None),
        P(("dp", "fsdp"), None),
        P(("dp", "fsdp"), None),
        P(("dp", "fsdp"), None),
        P(("dp", "fsdp"), None),
        P(("dp", "fsdp"), None),
        P(None, ("dp", "fsdp")),
        P(("dp", "fsdp")),
        P(("dp", "fsdp")),
        P(("dp", "fsdp")),
        P(("dp", "fsdp")),
        P(("dp", "fsdp")),
        P(("dp", "fsdp")),
        P(("dp", "fsdp")),
        P(("dp", "fsdp")),
        P(("dp", "fsdp")),
    )
    return jax.shard_map(
        local,
        mesh=mesh,
        in_specs=placed,
        out_specs=(
            P(None, ("dp", "fsdp"), None, None),
            P(None, ("dp", "fsdp"), None, None),
            P(("dp", "fsdp"), None),
            P(("dp", "fsdp"), None),
            P(("dp", "fsdp"), None),
            P(("dp", "fsdp"), None),
            P(("dp", "fsdp"), None),
            P(("dp", "fsdp"), None),
            P(None, ("dp", "fsdp")),
            P(("dp", "fsdp")),
            P(("dp", "fsdp")),
            P(("dp", "fsdp")),
            P(("dp", "fsdp")),
            P(("dp", "fsdp")),
            P(("dp", "fsdp")),
            P(("dp", "fsdp")),
            P(("dp", "fsdp")),
            P(("dp", "fsdp")),
        ),
        check_vma=False,
    )
```

profile of v0, /device:TPU:0, one launch (start us, length us, event | category | flops | bytes accessed | tf_op | source)
XLA Modules:
  0.0 1397.6 jit_solution(12687067983817451261)
XLA Ops:
  16.5 42.3 %all-reduce.19 = (bf16[512]{0:T(512)(128)(2,1)S(1)}, bf16[512]{0:T(512)(128)(2,1)S(1)}, bf16[512]{0:T(512)(128)(2,1)S(1)}, bf16[512]{0:T(512)(128)(2,1)S(1)}, bf...) all-reduce(bf16[512]{0:T(512)(128)(2,1)S(1)} %dynamic-update-slice,, ...), channel_id=1, replica_groups=mesh['dp'=4,'fsdp'=8] {'dp','fsdp'}, use_global_device_ids=true, to_apply=%add | all-reduce | flops 6144 | bytes 24576
  58.8 43.1 %all_gather.35 = bf16[512,512]{1,0:T(8,128)(2,1)S(1)} all-gather(bf16[16,512]{1,0:T(8,128)(2,1)} %param.22), channel_id=1, replica_groups=mesh['dp'=4,'fsdp'=8] {'dp','fsdp'}, dimensions={0}, use_global_device_ids=true | all-gather | bytes 540672 | tf_op jit(solution)/shard_map/all_gather | solution.py:241
  101.9 39.7 %all_gather.33 = bf16[512,512]{1,0:T(8,128)(2,1)S(1)} all-gather(bf16[16,512]{1,0:T(8,128)(2,1)} %param.24), channel_id=1, replica_groups=mesh['dp'=4,'fsdp'=8] {'dp','fsdp'}, dimensions={0}, use_global_device_ids=true | all-gather | bytes 540672 | tf_op jit(solution)/shard_map/all_gather | solution.py:243
  141.5 40.1 %all_gather.32 = bf16[512,512]{0,1:T(8,128)(2,1)S(1)} all-gather(bf16[512,16]{0,1:T(8,128)(2,1)} %param.28), channel_id=1, replica_groups=mesh['dp'=4,'fsdp'=8] {'dp','fsdp'}, dimensions={1}, use_global_device_ids=true | all-gather | bytes 540672 | tf_op jit(solution)/shard_map/all_gather | solution.py:247
  184.7 2.7 copy.194
  194.1 39.3 %all_gather.37 = bf16[512,512]{1,0:T(8,128)(2,1)S(1)} all-gather(bf16[16,512]{1,0:T(8,128)(2,1)S(1)} %copy-done.67), channel_id=1, replica_groups=mesh['dp'=4,'fsdp'=8] {'dp','fsdp'}, dimensions={0}, use_global_device_ids=true | all-gather | bytes 540672 | tf_op jit(solution)/shard_map/all_gather | solution.py:242
  235.0 42.3 %all_gather.38 = bf16[512,512]{1,0:T(8,128)(2,1)} all-gather(bf16[16,512]{1,0:T(8,128)(2,1)S(1)} %copy-done.68), channel_id=1, replica_groups=mesh['dp'=4,'fsdp'=8] {'dp','fsdp'}, dimensions={0}, use_global_device_ids=true | all-gather | bytes 540672 | tf_op jit(solution)/shard_map/all_gather | solution.py:244
  278.0 7.7 fusion.127
  285.8 8.4 fusion.1
  294.1 8.5 fusion.76
  302.6 7.5 fusion.129
  310.1 8.4 fusion
  318.5 9.0 fusion.77
  340.0 8.2 fusion.60
  348.2 7.7 multiply_convert_fusion.3
  355.9 8.8 fusion.132
  364.7 2.7 fusion.131
  368.1 2.3 fusion.39
  372.2 4.1 convert_reduce_fusion.2
  376.3 8.8 convert_reduce_fusion
  385.1 2.8 add_add_fusion.8
  387.9 11.8 convert_reduce_fusion.1
  399.7 7.3 multiply_reduce_fusion.3
  407.1 3.2 fusion.121
  414.8 5.2 convert_reduce_fusion.6
  420.0 9.7 multiply_reduce_fusion
  431.0 2.4 convert_reduce_fusion.5
  437.0 12.3 multiply_convert_fusion
  449.3 3.0 convert_reduce_fusion.8
  456.4 4.9 convert_reduce_fusion.7
  461.3 2.7 convolution_bitcast_fusion.2
  467.6 11.4 multiply_reduce_fusion.1
  479.1 11.9 multiply_convert_fusion.1
  496.2 6.2 multiply_convert_fusion.4
  504.0 2.6 multiply_convert_fusion.6
  519.9 5.4 fusion.116
  525.4 4.4 bitcast_add_fusion.1
  531.0 4.7 fusion.137
  535.7 10.0 bitcast_add_fusion
  548.5 2.4 copy.143
  551.2 38.7 %all-reduce.18 = (f32[512]{0:T(512)S(1)}, f32[512]{0:T(512)S(1)}, f32[512]{0:T(512)S(1)}, f32[2048]{0:T(1024)S(1)}, f32[512]{0:T(512)S(1)}, /*index=5*/f32[512]{...) all-reduce(f32[512]{0:T(512)S(1)} %add.358, ...), channel_id=9, replica_groups=mesh['dp'=4,'fsdp'=8] {'dp','fsdp'}, use_global_device_ids=true, to_apply=%region_33.34.clone | all-reduce | flops 6144 | bytes 49152
  595.9 2.4 copy.144
  598.9 105.1 %reduce-scatter.12.cloned.1.call-done = f32[16,512]{1,0:T(8,128)} async-done(((f32[512,512]{1,0:T(8,128)}), f32[16,512]{1,0:T(8,128)}) %reduce-scatter.12.cloned.1.call-update) | async-done | bytes 32784 | tf_op jit(solution)/shard_map/reduce_scatter | solution.py:292
  704.0 134.2 %reduce-scatter.8.cloned.1.call-done = f32[16,512]{1,0:T(8,128)} async-done(((f32[512,512]{1,0:T(8,128)}), f32[16,512]{1,0:T(8,128)}) %reduce-scatter.8.cloned.1.call-update) | async-done | bytes 32784 | tf_op jit(solution)/shard_map/reduce_scatter | solution.py:290
  838.2 134.4 %reduce-scatter.10.cloned.1.call-done = f32[16,512]{1,0:T(8,128)} async-done(((f32[512,512]{1,0:T(8,128)}), f32[16,512]{1,0:T(8,128)}) %reduce-scatter.10.cloned.1.call-update) | async-done | bytes 32784 | tf_op jit(solution)/shard_map/reduce_scatter | solution.py:291
  972.6 134.3 %reduce-scatter.20.cloned.1.call-done = f32[512,16]{0,1:T(8,128)} async-done(((f32[512,512]{0,1:T(8,128)}), f32[512,16]{0,1:T(8,128)}) %reduce-scatter.20.cloned.1.call-update) | async-done | bytes 32784 | tf_op jit(solution)/shard_map/reduce_scatter | solution.py:296
  1106.9 141.2 %reduce-scatter.16.cloned.1.call-done = f32[16,2048]{1,0:T(8,128)} async-done(((f32[512,2048]{1,0:T(8,128)}), f32[16,2048]{1,0:T(8,128)}) %reduce-scatter.16.cloned.1.call-update) | async-done | bytes 131088 | tf_op jit(solution)/shard_map/reduce_scatter | solution.py:294
  1248.2 142.4 %reduce-scatter.18.cloned.1.call-done = f32[64,512]{1,0:T(8,128)} async-done(((f32[2048,512]{1,0:T(8,128)}), f32[64,512]{1,0:T(8,128)}) %reduce-scatter.18.cloned.1.call-update) | async-done | bytes 131088 | tf_op jit(solution)/shard_map/reduce_scatter | solution.py:295
  (349 shorter events, 83.6 us)
Async XLA Ops:
  7.2 332.8 %all-gather.3.cloned.1.call-start = ((), (), s32[]{:S(2)}) async-start(), calls=%async_computation.7 | async-start | bytes 2162688 | tf_op jit(solution)/shard_map/all_gather | solution.py:245
  7.9 348.0 %all-gather.5.cloned.1.call-start = ((), (), s32[]{:S(2)}) async-start(), calls=%async_computation.8 | async-start | bytes 2162688 | tf_op jit(solution)/shard_map/all_gather | solution.py:246
  8.7 590.2 %reduce-scatter.14.cloned.1.call-start = ((), (), s32[]{:S(2)}) async-start(), calls=%async_computation.12 | async-start | bytes 1081344 | tf_op jit(solution)/shard_map/reduce_scatter | solution.py:293
  58.8 122.9 %copy-start.39 = (bf16[2,2,512,512]{3,2,1,0:T(8,128)(2,1)S(1)}, bf16[2,2,512,512]{3,2,1,0:T(8,128)(2,1)}, u32[]{:S(2)}) copy-start(bf16[2,2,512,512]{3,2,1,0:T(8,128)(2,1)} %param.19) | copy-start | bytes 6291460
  101.9 87.9 %copy-start.23 = (bf16[512,512]{1,0:T(8,128)(2,1)}, bf16[512,512]{1,0:T(8,128)(2,1)S(1)}, u32[]{:S(2)}) copy-start(bf16[512,512]{1,0:T(8,128)(2,1)S(1)} %all_gather.35) | copy-start | bytes 1572868
  141.5 50.8 %copy-start.21 = (bf16[512,512]{1,0:T(8,128)(2,1)}, bf16[512,512]{1,0:T(8,128)(2,1)S(1)}, u32[]{:S(2)}) copy-start(bf16[512,512]{1,0:T(8,128)(2,1)S(1)} %all_gather.33) | copy-start | bytes 1572868
  189.0 44.4 %copy-start.6 = (bf16[2,512,512]{1,2,0:T(8,128)(2,1)}, bf16[2,512,512]{1,2,0:T(8,128)(2,1)S(1)}, u32[]{:S(2)}) copy-start(bf16[2,512,512]{1,2,0:T(8,128)(2,1)S(1)} %get-tuple-element.112) | copy-start | bytes 3145732
  189.0 45.1 %copy-start.41 = (bf16[2,512,512]{1,2,0:T(8,128)(2,1)}, bf16[2,512,512]{1,2,0:T(8,128)(2,1)S(1)}, u32[]{:S(2)}) copy-start(bf16[2,512,512]{1,2,0:T(8,128)(2,1)S(1)} %get-tuple-element.113) | copy-start | bytes 3145732
  189.8 112.8 %copy-start.27 = (bf16[2,512,512]{1,2,0:T(8,128)(2,1)}, bf16[2,512,512]{1,2,0:T(8,128)(2,1)S(1)}, u32[]{:S(2)}) copy-start(bf16[2,512,512]{1,2,0:T(8,128)(2,1)S(1)} %add_convert_fusion.4) | copy-start | bytes 3145732
  190.6 87.5 %copy-start.29 = (bf16[2,512,512]{1,2,0:T(8,128)(2,1)}, bf16[2,512,512]{1,2,0:T(8,128)(2,1)S(1)}, u32[]{:S(2)}) copy-start(bf16[2,512,512]{1,2,0:T(8,128)(2,1)S(1)} %add_convert_fusion.1) | copy-start | bytes 3145732
  234.2 68.5 %copy-start.15 = (bf16[2,512,512]{1,2,0:T(8,128)(2,1)}, bf16[2,512,512]{1,2,0:T(8,128)(2,1)S(1)}, u32[]{:S(2)}) copy-start(bf16[2,512,512]{1,2,0:T(8,128)(2,1)S(1)} %convolution_convert_fusion.3) | copy-start | bytes 3145732
  235.0 50.8 %copy-start.17 = (bf16[2,512,512]{1,2,0:T(8,128)(2,1)}, bf16[2,512,512]{1,2,0:T(8,128)(2,1)S(1)}, u32[]{:S(2)}) copy-start(bf16[2,512,512]{1,2,0:T(8,128)(2,1)S(1)} %convolution_convert_fusion.2) | copy-start | bytes 3145732
  285.8 8.4 copy-start.49
  310.1 8.4 copy-start.44
  318.5 9.0 copy-start.34
  318.5 9.0 copy-start.54
  318.5 9.0 copy-start.95
  330.9 76.2 %copy-start.83 = (f32[512]{0:T(512)}, f32[512]{0:T(512)S(1)}, u32[]{:S(2)}) copy-start(f32[512]{0:T(512)S(1)} %convert_element_type.263) | copy-start | bytes 6148
  330.9 33.8 %copy-start.89 = (f32[512]{0:T(512)}, f32[512]{0:T(512)S(1)}, u32[]{:S(2)}) copy-start(f32[512]{0:T(512)S(1)} %convert_element_type.264) | copy-start | bytes 6148
  330.9 56.9 %copy-start.77 = (f32[2048]{0:T(1024)}, f32[2048]{0:T(1024)S(1)}, u32[]{:S(2)}) copy-start(f32[2048]{0:T(1024)S(1)} %convert_element_type.266) | copy-start | bytes 24580
  338.6 68.4 %copy-start.63 = (f32[2,512]{1,0:T(2,128)}, f32[2,512]{1,0:T(2,128)S(1)}, u32[]{:S(2)}) copy-start(f32[2,512]{1,0:T(2,128)S(1)} %fusion.112) | copy-start | bytes 12292
  338.7 68.4 %copy-start.65 = (f32[2,512]{1,0:T(2,128)}, f32[2,512]{1,0:T(2,128)S(1)}, u32[]{:S(2)}) copy-start(f32[2,512]{1,0:T(2,128)S(1)} %fusion.110) | copy-start | bytes 12292
  340.0 8.2 copy-start.13
  340.0 8.2 copy-start.92
  355.9 8.8 copy-start.14
  355.9 8.8 copy-start.94
  355.9 8.8 copy-start.99
  368.1 8.2 slice-start.8
  376.3 8.8 copy-start.45
  376.3 11.6 copy-start.47
  376.3 8.8 copy-start.93
  387.9 11.8 copy-start.10
  399.7 15.0 %slice-start.4 = ((s8[16777216]{0:T(1024)(128)(4,1)}), s8[4194304]{0:T(1024)(128)(4,1)S(1)}, s32[]{:S(2)}) async-start(s8[16777216]{0:T(1024)(128)(4,1)} %bitcast.264), calls=%async_computation.20 | async-start | bytes 8388608
  399.7 15.0 %slice-start.5 = ((s8[16777216]{0:T(1024)(128)(4,1)}), s8[4194304]{0:T(1024)(128)(4,1)S(1)}, s32[]{:S(2)}) async-start(s8[16777216]{0:T(1024)(128)(4,1)} %bitcast.264), calls=%async_computation.21 | async-start | bytes 8388608
  399.7 15.0 %slice-start.6 = ((s8[16777216]{0:T(1024)(128)(4,1)}), s8[4194304]{0:T(1024)(128)(4,1)S(1)}, s32[]{:S(2)}) async-start(s8[16777216]{0:T(1024)(128)(4,1)} %bitcast.264), calls=%async_computation.22 | async-start | bytes 8388608
  407.1 7.7 slice-start.7
  436.9 267.2 %reduce-scatter.12.cloned.1.call-start = ((), (), s32[]{:S(2)}) async-start(), calls=%async_computation.11 | async-start | bytes 1081344 | tf_op jit(solution)/shard_map/reduce_scatter | solution.py:292
  436.9 12.4 copy-start.18
  436.9 17.1 %slice-start = ((s8[16777216]{0:T(1024)(128)(4,1)}), s8[4194304]{0:T(1024)(128)(4,1)S(1)}, s32[]{:S(2)}) async-start(s8[16777216]{0:T(1024)(128)(4,1)} %bitcast.262), calls=%async_computation.16 | async-start | bytes 8388608
  436.9 17.1 %slice-start.1 = ((s8[16777216]{0:T(1024)(128)(4,1)}), s8[4194304]{0:T(1024)(128)(4,1)S(1)}, s32[]{:S(2)}) async-start(s8[16777216]{0:T(1024)(128)(4,1)} %bitcast.262), calls=%async_computation.17 | async-start | bytes 8388608
  437.0 17.7 %slice-start.2 = ((s8[16777216]{0:T(1024)(128)(4,1)}), s8[4194304]{0:T(1024)(128)(4,1)S(1)}, s32[]{:S(2)}) async-start(s8[16777216]{0:T(1024)(128)(4,1)} %bitcast.262), calls=%async_computation.18 | async-start | bytes 8388608
  479.0 359.2 %reduce-scatter.8.cloned.1.call-start = ((), (), s32[]{:S(2)}) async-start(), calls=%async_computation.9 | async-start | bytes 1081344 | tf_op jit(solution)/shard_map/reduce_scatter | solution.py:290
  479.1 11.9 copy-start.16
  495.9 476.6 %reduce-scatter.10.cloned.1.call-start = ((), (), s32[]{:S(2)}) async-start(), calls=%async_computation.10 | async-start | bytes 1081344 | tf_op jit(solution)/shard_map/reduce_scatter | solution.py:291
  508.4 598.5 %reduce-scatter.20.cloned.1.call-start = ((), (), s32[]{:S(2)}) async-start(), calls=%async_computation.15 | async-start | bytes 1081344 | tf_op jit(solution)/shard_map/reduce_scatter | solution.py:296
  519.8 728.3 %reduce-scatter.16.cloned.1.call-start = ((), (), s32[]{:S(2)}) async-start(), calls=%async_computation.13 | async-start | bytes 4325376 | tf_op jit(solution)/shard_map/reduce_scatter | solution.py:294
  529.9 860.7 %reduce-scatter.18.cloned.1.call-start = ((), (), s32[]{:S(2)}) async-start(), calls=%async_computation.14 | async-start | bytes 4325376 | tf_op jit(solution)/shard_map/reduce_scatter | solution.py:295
  548.5 46.0 %copy-start.36 = (bf16[1,2,512,512]{2,3,1,0:T(8,128)(2,1)S(1)}, bf16[1,2,512,512]{2,3,1,0:T(8,128)(2,1)}, u32[]{:S(2)}) copy-start(bf16[1,2,512,512]{2,3,1,0:T(8,128)(2,1)} %get-tuple-element.105) | copy-start | bytes 3145732
  (71 other events, 190.7 us)
Sparse Core Ops, SparseCore 0:
  11.0 59.2 all-gather.2
  73.3 56.4 all-gather.4
  437.0 132.4 reduce-scatter.13
  572.3 131.6 reduce-scatter.11
  706.7 131.4 reduce-scatter.7
  841.0 131.5 reduce-scatter.9
  975.4 131.4 reduce-scatter.19
  1109.9 138.2 reduce-scatter.15
  1251.1 139.4 reduce-scatter.17
where the time goes:
time: 1410 us; the launch traced here: 1400 us
  waiting for transfers between devices  793 us (56%)
  blocking collectives  285 us (20%)
  matrix products  195 us (14%)
  other arithmetic  67.2 us (5%)
  local copies, waits for them, and re-layouts  40.4 us (3%)
  between operations  15.8 us (1%)
    reduce_scatter x1, waiting for transfers between devices, local(): lax.psum_scatter(accumulated[5], ('dp', 'fsdp'), scatter_dimension=0, til...  142 us
    reduce_scatter x1, waiting for transfers between devices, local(): lax.psum_scatter(accumulated[4], ('dp', 'fsdp'), scatter_dimension=0, til...  141 us
    reduce_scatter x1, waiting for transfers between devices, local(): lax.psum_scatter(accumulated[1], ('dp', 'fsdp'), scatter_dimension=0, til...  134 us
    reduce_scatter x1, waiting for transfers between devices, local(): lax.psum_scatter(accumulated[6], ('dp', 'fsdp'), scatter_dimension=1, til...  134 us
    reduce_scatter x1, waiting for transfers between devices, local(): lax.psum_scatter(accumulated[0], ('dp', 'fsdp'), scatter_dimension=0, til...  134 us
    reduce_scatter x1, waiting for transfers between devices, local(): lax.psum_scatter(accumulated[2], ('dp', 'fsdp'), scatter_dimension=0, til...  105 us
    unnamed x2, blocking collectives  81 us
    all_gather x1, blocking collectives, local(): lax.all_gather(query_weight, ('dp', 'fsdp'), axis=0, tiled=True)  43.1 us
  transfers between devices with their start and end apart: 9, of which 6 were waited for; matrix products, arithmetic and copies ran while one was open for 15% of the time, Pallas kernels for 0%

commit v1 on v0

v1 whole, which is shorter than its diff:
```python
import functools
import jax, jax.numpy as jnp
from jax import lax
from jax.experimental import pallas as pl
from jax.experimental.pallas import tpu as pltpu
from jax.sharding import PartitionSpec as P

HEADS = 8
EPS = 1e-05
BF = jnp.bfloat16
F32 = jnp.float32
GELU_C = 0.7978845608028654
GELU_A = 0.044715


def nn(a, b):
    return lax.dot_general(a, b, (((1,), (0,)), ((), ())), preferred_element_type=F32)


def nt(a, b):
    return lax.dot_general(a, b, (((1,), (1,)), ((), ())), preferred_element_type=F32)


def tn(a, b):
    return lax.dot_general(a, b, (((0,), (0,)), ((), ())), preferred_element_type=F32)


def rows_of(vec, index):
    return vec[index : index + 1, :]


(BQ, BV, BM, BS, G1, S1, G2, S2) = range(8)


def attention_forward(w, r):
    seq, width = r.x.shape[1:]
    half = seq // 2
    head = width // HEADS
    hid = r.x[w].astype(F32) + r.pos[...].astype(F32)
    low = hid.astype(BF)
    r.low[w] = low
    r.q[w] = (((nn(low, r.wq[...]) + r.vec[BQ : BQ + 1, :]).astype(BF)).astype(F32) * (head**-0.5)).astype(BF)
    r.k[w] = nn(low, r.wk[...]).astype(BF)
    values = (nn(low, r.wv[...]) + r.vec[BV : BV + 1, :]).astype(BF)
    r.v[w] = values
    r.vt[...] = values.T
    make_mask(w, r)
    lane = lax.broadcasted_iota(jnp.int32, (seq, 2 * head), 1)
    for h in range(HEADS):
        pair = slice((h // 2) * 2 * head, (h // 2 + 1) * 2 * head)
        mine = (lane < head) if h % 2 == 0 else (lane >= head)
        qh = jnp.where(mine, r.q[w, :, pair], jnp.zeros((), BF))
        kp = r.k[w, :, pair]
        s0 = nt(kp[:half], qh) + r.mask[:half, :]
        s1 = nt(kp[half:], qh[half:]) + r.mask[half:, half:]
        m_left = jnp.max(s0[:, :half], axis=0, keepdims=True)
        m_right = jnp.maximum(
            jnp.max(s0[:, half:], axis=0, keepdims=True), jnp.max(s1, axis=0, keepdims=True)
        )
        top = jnp.concatenate([m_left, m_right], axis=1)
        e0 = jnp.exp(s0 - top)
        e1 = jnp.exp(s1 - m_right)
        n_all = jnp.sum(e0, axis=0, keepdims=True)
        n_right = n_all[:, half:] + jnp.sum(e1, axis=0, keepdims=True)
        total = jnp.concatenate([n_all[:, :half], n_right], axis=1)
        r.logt[w, h : h + 1, :] = top + jnp.log(total)
        inv = 1.0 / total
        p0 = (e0 * inv).astype(BF)
        p1 = (e1 * inv[:, half:]).astype(BF)
        vt = r.vt[h * head : (h + 1) * head, :]
        o_left = nn(vt[:, :half], p0[:, :half])
        o_right = nn(vt, jnp.concatenate([p0[:, half:], p1], axis=0))
        r.ot[h * head : (h + 1) * head, :half] = o_left.astype(BF)
        r.ot[h * head : (h + 1) * head, half:] = o_right.astype(BF)
    r.mixed[w] = r.ot[...].T


def make_mask(w, r):
    seq = r.x.shape[1]
    key_at = lax.broadcasted_iota(jnp.int32, (seq, seq), 0)
    query_at = lax.broadcasted_iota(jnp.int32, (seq, seq), 1)
    ok = (key_at <= query_at) & (key_at < r.lens[w])
    r.mask[...] = jnp.where(ok, 0.0, -1e30)


def norm_parts(total):
    center = total - jnp.mean(total, -1, keepdims=True)
    spread = jnp.mean(center * center, -1, keepdims=True)
    inv = lax.rsqrt(spread + EPS)
    return center * inv, inv


def norm_back(e, xhat, inv):
    return inv * (
        e - jnp.mean(e, -1, keepdims=True) - xhat * jnp.mean(e * xhat, -1, keepdims=True)
    )


def add_row(ref, index, value):
    ref[index : index + 1, :] += jnp.sum(value, axis=0, keepdims=True)


def feed_forward(w, r):
    seq, width = r.x.shape[1:]
    ff = r.we.shape[1]
    chunk = 512
    hid = r.x[w].astype(F32) + r.pos[...].astype(F32)
    mixed = r.mixed[w]
    first = hid + (nn(mixed, r.wm[...]) + r.vec[BM : BM + 1, :])
    xhat1, inv1 = norm_parts(first)
    r.xh1[...] = xhat1
    normed = xhat1 * r.vec[G1 : G1 + 1, :] + r.vec[S1 : S1 + 1, :]
    r.nl[...] = normed.astype(BF)
    ff_out = None
    for c in range(ff // chunk):
        cols = slice(c * chunk, (c + 1) * chunk)
        t = nn(r.nl[...], r.we[:, cols]) + r.eb[:, cols]
        t2 = t * t
        th = jnp.tanh(t * (t2 * (GELU_A * GELU_C) + GELU_C))
        ht = 0.5 * t
        act = (ht * th + ht).astype(BF)
        r.act[:, cols] = act
        slope = (0.5 * th + 0.5) + ht * (1.0 - th * th) * (t2 * (3 * GELU_A * GELU_C) + GELU_C)
        r.slope[:, cols] = slope
        part = nn(act, r.ws[cols, :])
        ff_out = part if ff_out is None else ff_out + part
    second = normed + (ff_out + r.vec[BS : BS + 1, :])
    xhat2, inv2 = norm_parts(second)
    r.out[w] = (xhat2 * r.vec[G2 : G2 + 1, :] + r.vec[S2 : S2 + 1, :]).astype(BF)
    row_at = lax.broadcasted_iota(jnp.int32, (seq, width), 0)
    cot = jnp.where(row_at < r.lens[w], r.go[w].astype(F32), 0.0)
    add_row(r.gvec, G2, cot * xhat2)
    add_row(r.gvec, S2, cot)
    d_second = norm_back(cot * r.vec[G2 : G2 + 1, :], xhat2, inv2)
    gff = d_second.astype(BF)
    r.gff[...] = gff
    add_row(r.gvec, BS, gff.astype(F32))
    d_normed = d_second
    for c in range(ff // chunk):
        cols = slice(c * chunk, (c + 1) * chunk)
        gpre = (nt(r.gff[...], r.ws[cols, :]) * r.slope[:, cols]).astype(BF)
        add_row_cols(r.geb, cols, gpre.astype(F32))
        r.gws[cols, :] += tn(r.act[:, cols], r.gff[...])
        r.gwe[:, cols] += tn(r.nl[...], gpre)
        d_normed = d_normed + nt(gpre, r.we[:, cols])
    xhat1 = r.xh1[...]
    add_row(r.gvec, G1, d_normed * xhat1)
    add_row(r.gvec, S1, d_normed)
    d_first = norm_back(d_normed * r.vec[G1 : G1 + 1, :], xhat1, inv1)
    r.dfirst[w] = d_first
    gattn = d_first.astype(BF)
    add_row(r.gvec, BM, gattn.astype(F32))
    r.gwm[...] += tn(mixed, gattn)
    gmix = nt(gattn, r.wm[...]).astype(BF)
    head = width // HEADS
    prod = gmix.astype(F32) * mixed.astype(F32)
    hi = prod.astype(BF)
    lo = (prod - hi.astype(F32)).astype(BF)
    sel_row = lax.broadcasted_iota(jnp.int32, (16, width), 0)
    sel_col = lax.broadcasted_iota(jnp.int32, (16, width), 1)
    sel = jnp.where(sel_col // head == sel_row, 1.0, 0.0).astype(BF)
    r.delta[w] = nt(sel, hi) + nt(sel, lo)
    r.mixed[w] = gmix


def add_row_cols(ref, cols, value):
    ref[:, cols] += jnp.sum(value, axis=0, keepdims=True)


def attention_backward(w, r):
    seq, width = r.x.shape[1:]
    half = seq // 2
    head = width // HEADS
    scale = head**-0.5
    make_mask(w, r)
    r.kt[...] = r.k[w].T
    lane = lax.broadcasted_iota(jnp.int32, (seq, 2 * head), 1)
    for p in range(HEADS // 2):
        pair = slice(p * 2 * head, (p + 1) * 2 * head)
        kp = r.k[w, :, pair]
        vp = r.v[w, :, pair]
        dk_top = dk_low = dv_top = dv_low = None
        for odd in range(2):
            h = 2 * p + odd
            mine = (lane >= head) if odd else (lane < head)
            qh = jnp.where(mine, r.q[w, :, pair], jnp.zeros((), BF))
            gh = jnp.where(mine, r.mixed[w, :, pair], jnp.zeros((), BF))
            logt = r.logt[w, h : h + 1, :]
            delta = r.delta[w, h : h + 1, :]
            p0 = jnp.exp(nt(kp[:half], qh) + r.mask[:half, :] - logt)
            p1 = jnp.exp(nt(kp[half:], qh[half:]) + r.mask[half:, half:] - logt[:, half:])
            d0 = (p0 * (nt(vp[:half], gh) - delta)).astype(BF)
            d1 = (p1 * (nt(vp[half:], gh[half:]) - delta[:, half:])).astype(BF)
            p0 = p0.astype(BF)
            p1 = p1.astype(BF)
            parts = (nn(d0, qh), nn(d1, qh[half:]), nn(p0, gh), nn(p1, gh[half:]))
            if odd:
                dk_top, dk_low, dv_top, dv_low = (
                    first + second for first, second in zip((dk_top, dk_low, dv_top, dv_low), parts)
                )
            else:
                dk_top, dk_low, dv_top, dv_low = parts
            kt = r.kt[h * head : (h + 1) * head, :]
            q_left = nn(kt[:, :half], d0[:, :half])
            q_right = nn(kt, jnp.concatenate([d0[:, half:], d1], axis=0))
            r.ot[h * head : (h + 1) * head, :half] = (q_left * scale).astype(BF)
            r.ot[h * head : (h + 1) * head, half:] = (q_right * scale).astype(BF)
        r.gk[:half, pair] = dk_top.astype(BF)
        r.gk[half:, pair] = dk_low.astype(BF)
        r.gv[:half, pair] = dv_top.astype(BF)
        r.gv[half:, pair] = dv_low.astype(BF)
    gq = r.ot[...].T
    gk = r.gk[...]
    gv = r.gv[...]
    low = r.low[w]
    r.gwq[...] += tn(low, gq)
    r.gwk[...] += tn(low, gk)
    r.gwv[...] += tn(low, gv)
    add_row(r.gvec, BQ, gq.astype(F32))
    add_row(r.gvec, BV, gv.astype(F32))
    d_hidden = r.dfirst[w] + nt(gq, r.wq[...]) + nt(gk, r.wk[...]) + nt(gv, r.wv[...])
    r.gpos[...] += d_hidden
    r.gin[w] = d_hidden.astype(BF)


class Refs:
    def __init__(self, **kw):
        self.__dict__.update(kw)


IN_NAMES = ("lens", "x", "go", "wq", "wk", "wv", "wm", "we", "ws", "pos", "vec", "eb")
OUT_NAMES = ("out", "gin", "gwq", "gwk", "gwv", "gwm", "gwe", "gws", "gpos", "gvec", "geb")


def scratch_list(count, seq, width, ff):
    return dict(
        low=pltpu.VMEM((count, seq, width), BF),
        q=pltpu.VMEM((count, seq, width), BF),
        k=pltpu.VMEM((count, seq, width), BF),
        v=pltpu.VMEM((count, seq, width), BF),
        mixed=pltpu.VMEM((count, seq, width), BF),
        logt=pltpu.VMEM((count, HEADS, seq), F32),
        delta=pltpu.VMEM((count, 16, seq), F32),
        dfirst=pltpu.VMEM((count, seq, width), F32),
        vt=pltpu.VMEM((width, seq), BF),
        kt=pltpu.VMEM((width, seq), BF),
        ot=pltpu.VMEM((width, seq), BF),
        gk=pltpu.VMEM((seq, width), BF),
        gv=pltpu.VMEM((seq, width), BF),
        mask=pltpu.VMEM((seq, seq), F32),
        xh1=pltpu.VMEM((seq, width), F32),
        nl=pltpu.VMEM((seq, width), BF),
        gff=pltpu.VMEM((seq, width), BF),
        act=pltpu.VMEM((seq, ff), BF),
        slope=pltpu.VMEM((seq, ff), F32),
    )


def compute_kernel(names, phases, *refs):
    r = Refs(**dict(zip(names, refs)))
    for name in OUT_NAMES[2:]:
        ref = getattr(r, name)
        ref[...] = jnp.zeros(ref.shape, ref.dtype)
    count = r.x.shape[0]
    def loop(fn):
        def body(w, c):
            fn(w, r)
            return c
        lax.fori_loop(0, count, body, 0)
    if 1 in phases: loop(attention_forward)
    if 2 in phases: loop(feed_forward)
    if 3 in phases: loop(attention_backward)


def compute(lens, x, go, wq, wk, wv, wm, we, ws, pos, vec, eb, phases=(1, 2, 3)):
    count, seq, width = x.shape
    ff = we.shape[1]
    scr = scratch_list(count, seq, width, ff)
    S = jax.ShapeDtypeStruct
    outs = (
        S((count, seq, width), BF), S((count, seq, width), BF),
        S((width, width), F32), S((width, width), F32), S((width, width), F32), S((width, width), F32),
        S((width, ff), F32), S((ff, width), F32), S((seq, width), F32), S((8, width), F32), S((1, ff), F32),
    )
    names = IN_NAMES + OUT_NAMES + tuple(scr)
    vm = pl.BlockSpec(memory_space=pltpu.VMEM)
    return pl.pallas_call(
        functools.partial(compute_kernel, names, phases),
        out_shape=outs,
        in_specs=[pl.BlockSpec(memory_space=pltpu.SMEM)] + [vm] * (len(IN_NAMES) - 1),
        out_specs=[vm] * len(outs),
        scratch_shapes=list(scr.values()),
        compiler_params=pltpu.CompilerParams(vmem_limit_bytes=63 * 2**20),
        name="layer",
    )(lens, x, go, wq, wk, wv, wm, we, ws, pos, vec, eb)


MESH = pl.DeviceIdType.MESH


class Place:
    def __init__(self, dp_count, z_count):
        self.dp_count, self.z_count = dp_count, z_count
        self.dp = lax.axis_index("dp")
        fsdp = lax.axis_index("fsdp")
        self.z, self.c = fsdp // 2, lax.rem(fsdp, 2)

    def z_at(self, shift):
        return lax.rem(self.z + shift + self.z_count, self.z_count)

    def dp_at(self, shift):
        return lax.rem(self.dp + shift + self.dp_count, self.dp_count)

    def peers(self):
        near = [(self.dp, self.z * 2 + (1 - self.c))]
        along_z = [(self.dp, self.z_at(s) * 2 + self.c) for s in range(1, self.z_count)]
        along_dp = [(self.dp_at(s), self.z * 2 + self.c) for s in range(1, self.dp_count)]
        return near, along_z, along_dp

    def barrier(self):
        sem = pltpu.get_barrier_semaphore()
        near, along_z, along_dp = self.peers()
        everyone = near + along_z + along_dp
        for peer in everyone:
            pl.semaphore_signal(sem, inc=1, device_id=peer, device_id_type=MESH)
        pl.semaphore_wait(sem, len(everyone))


def remote(src, dst, sems, index, peer):
    send, recv = sems
    return pltpu.make_async_remote_copy(
        src_ref=src, dst_ref=dst, send_sem=send.at[index], recv_sem=recv.at[index],
        device_id=peer, device_id_type=MESH,
    )


class Gather:
    def __init__(self, place, shard, whole, sems):
        self.p, self.shard, self.whole, self.sems = place, shard, whole, sems
        self.near, self.along_z, self.along_dp = place.peers()

    def z_copy(self, shift, z):
        p = self.p
        return remote(self.shard, self.whole.at[p.dp, z, p.c], self.sems, shift - 1, self.along_z[shift - 1])

    def dp_copy(self, shift, dp):
        p = self.p
        at = self.p.z_count - 1 + shift - 1
        return remote(self.whole.at[p.dp, :, p.c], self.whole.at[dp, :, p.c], self.sems, at, self.along_dp[shift - 1])

    def core_copy(self, core):
        at = self.p.z_count + self.p.dp_count - 2
        return remote(self.whole.at[:, :, self.p.c], self.whole.at[:, :, core], self.sems, at, self.near[0])

    def start_z(self):
        p = self.p
        for shift in range(1, p.z_count):
            self.z_copy(shift, p.z).start()
        self.whole[p.dp, p.z, p.c] = self.shard[...]

    def start_dp(self):
        p = self.p
        for shift in range(1, p.z_count):
            self.z_copy(shift, p.z_at(-shift)).wait_recv()
        for shift in range(1, p.dp_count):
            self.dp_copy(shift, p.dp).start()

    def start_core(self):
        p = self.p
        for shift in range(1, p.dp_count):
            self.dp_copy(shift, p.dp_at(-shift)).wait_recv()
        self.core_copy(p.c).start()

    def finish(self):
        self.core_copy(1 - self.p.c).wait_recv()

    def drain(self):
        p = self.p
        for shift in range(1, p.z_count):
            self.z_copy(shift, p.z).wait_send()
        for shift in range(1, p.dp_count):
            self.dp_copy(shift, p.dp).wait_send()
        self.core_copy(p.c).wait_send()


class Scatter:
    def __init__(self, place, total, result, bufs, sems):
        self.p, self.total, self.result, self.sems = place, total, result, sems
        self.to_core, self.from_core, self.to_dp, self.from_dp, self.from_z, self.own = bufs
        self.near, self.along_z, self.along_dp = place.peers()

    def core_copy(self):
        at = self.p.z_count + self.p.dp_count - 2
        return remote(self.to_core, self.from_core, self.sems, at, self.near[0])

    def dp_copy(self, shift):
        at = self.p.z_count - 1 + shift - 1
        return remote(self.to_dp.at[self.p.dp_at(shift)], self.from_dp.at[shift - 1], self.sems, at, self.along_dp[shift - 1])

    def z_copy(self, shift):
        return remote(self.to_dp.at[self.p.dp, self.p.z_at(shift)], self.from_z.at[shift - 1], self.sems, shift - 1, self.along_z[shift - 1])

    def start_core(self):
        self.to_core[...] = self.total[:, :, 1 - self.p.c].astype(BF)
        self.core_copy().start()

    def start_dp(self):
        p = self.p
        self.core_copy().wait_recv()
        both = self.total[:, :, p.c] + self.from_core[...].astype(F32)
        self.to_dp[...] = both.astype(BF)
        for shift in range(1, p.dp_count):
            self.dp_copy(shift).start()
        self.own[...] = self.total[p.dp, :, p.c] + self.from_core[p.dp].astype(F32)

    def start_z(self):
        p = self.p
        for shift in range(1, p.dp_count):
            self.dp_copy(shift).wait_recv()
        added = self.own[...]
        for shift in range(1, p.dp_count):
            added = added + self.from_dp[shift - 1].astype(F32)
        self.own[...] = added
        self.to_dp[p.dp] = added.astype(BF)
        for shift in range(1, p.z_count):
            self.z_copy(shift).start()

    def finish(self):
        p = self.p
        for shift in range(1, p.z_count):
            self.z_copy(shift).wait_recv()
        added = self.own[p.z]
        for shift in range(1, p.z_count):
            added = added + self.from_z[shift - 1].astype(F32)
        self.result[...] = added

    def drain(self):
        p = self.p
        self.core_copy().wait_send()
        for shift in range(1, p.dp_count):
            self.dp_copy(shift).wait_send()
        for shift in range(1, p.z_count):
            self.z_copy(shift).wait_send()


class SumAll:
    def __init__(self, place, total, bufs, sems):
        self.p, self.total, self.sems = place, total, sems
        self.send_dp, self.send_z, self.landing = bufs
        self.near, self.along_z, self.along_dp = place.peers()

    def copies(self, hop):
        p = self.p
        z, dp = p.z_count - 1, p.dp_count - 1
        if hop == 0:
            return [remote(self.total, self.landing.at[z + dp], self.sems, z + dp, self.near[0])]
        if hop == 1:
            return [remote(self.send_dp, self.landing.at[z + s], self.sems, z + s, self.along_dp[s]) for s in range(dp)]
        return [remote(self.send_z, self.landing.at[s], self.sems, s, self.along_z[s]) for s in range(z)]

    def arrived(self, hop, first):
        for copy in self.copies(hop):
            copy.wait_recv()
        z, dp = self.p.z_count - 1, self.p.dp_count - 1
        slots = ([z + dp], range(z, z + dp), range(z))[hop]
        added = first[...]
        for slot in slots:
            added = added + self.landing[slot]
        return added

    def start_core(self):
        self.copies(0)[0].start()

    def start_dp(self):
        self.send_dp[...] = self.arrived(0, self.total)
        for copy in self.copies(1):
            copy.start()

    def start_z(self):
        self.send_z[...] = self.arrived(1, self.send_dp)
        for copy in self.copies(2):
            copy.start()

    def finish(self, result):
        result[...] = self.arrived(2, self.send_z)

    def drain(self):
        for hop in range(3):
            for copy in self.copies(hop):
                copy.wait_send()


def sem_pair(place_counts):
    dp_count, z_count = place_counts
    hops = dp_count + z_count - 1
    return [pltpu.SemaphoreType.DMA((hops,)), pltpu.SemaphoreType.DMA((hops,))]


AXES = ("dp", "fsdp")
LANES = 128


def gather_kernel(counts, tensors, *refs):
    shards, wholes, sems = refs[:tensors], refs[tensors : 2 * tensors], refs[2 * tensors :]
    place = Place(*counts)
    place.barrier()
    gathers = [
        Gather(place, shard, whole, (sems[2 * i], sems[2 * i + 1]))
        for i, (shard, whole) in enumerate(zip(shards, wholes))
    ]
    for step in ("start_z", "start_dp", "start_core", "finish", "drain"):
        for gather in gathers:
            getattr(gather, step)()


def gather_all(counts, shards):
    dp_count, z_count = counts
    vm = pl.BlockSpec(memory_space=pltpu.VMEM)
    outs = pl.pallas_call(
        functools.partial(gather_kernel, counts, len(shards)),
        out_shape=tuple(
            jax.ShapeDtypeStruct((dp_count, z_count, 2) + shard.shape, shard.dtype) for shard in shards
        ),
        in_specs=[vm] * len(shards),
        out_specs=[vm] * len(shards),
        scratch_shapes=sum([sem_pair(counts) for _ in shards], []),
        compiler_params=pltpu.CompilerParams(
            collective_id=0, has_side_effects=True, vmem_limit_bytes=60 * 2**20
        ),
        name="gather",
    )(*shards)
    return [out.reshape((-1,) + out.shape[4:]) for out in outs]


def scatter_kernel(counts, tensors, *refs):
    totals, small = refs[:tensors], refs[tensors]
    results, small_result = refs[tensors + 1 : 2 * tensors + 1], refs[2 * tensors + 1]
    rest = list(refs[2 * tensors + 2 :])
    place = Place(*counts)
    place.barrier()
    jobs = []
    for total, result in zip(totals, results):
        bufs, sems, rest = rest[:6], rest[6:8], rest[8:]
        jobs.append(Scatter(place, total, result, bufs, sems))
    sums = SumAll(place, small, rest[:3], rest[3:5])
    for step in ("start_core", "start_dp", "start_z"):
        for job in jobs:
            getattr(job, step)()
        getattr(sums, step)()
    for job in jobs:
        job.finish()
    sums.finish(small_result)
    for job in jobs + [sums]:
        job.drain()


def scatter_bufs(counts, shape):
    dp_count, z_count = counts
    return [
        pltpu.VMEM((dp_count, z_count) + shape, BF),
        pltpu.VMEM((dp_count, z_count) + shape, BF),
        pltpu.VMEM((dp_count, z_count) + shape, BF),
        pltpu.VMEM((dp_count - 1, z_count) + shape, BF),
        pltpu.VMEM((z_count - 1,) + shape, BF),
        pltpu.VMEM((z_count,) + shape, F32),
    ]


def scatter_all(counts, totals, small):
    dp_count, z_count = counts
    devices = dp_count * z_count * 2
    vm = pl.BlockSpec(memory_space=pltpu.VMEM)
    totals = [total.reshape((dp_count, z_count, 2, -1) + total.shape[1:]) for total in totals]
    shapes = [total.shape[3:] for total in totals]
    scratch = []
    for shape in shapes:
        scratch += scatter_bufs(counts, shape) + sem_pair(counts)
    hops = dp_count + z_count - 1
    scratch += [pltpu.VMEM(small.shape, F32), pltpu.VMEM(small.shape, F32), pltpu.VMEM((hops,) + small.shape, F32)]
    scratch += sem_pair(counts)
    return pl.pallas_call(
        functools.partial(scatter_kernel, counts, len(totals)),
        out_shape=tuple(jax.ShapeDtypeStruct(shape, F32) for shape in shapes)
        + (jax.ShapeDtypeStruct(small.shape, F32),),
        in_specs=[vm] * (len(totals) + 1),
        out_specs=[vm] * (len(totals) + 1),
        scratch_shapes=scratch,
        compiler_params=pltpu.CompilerParams(
            collective_id=1, has_side_effects=True, vmem_limit_bytes=60 * 2**20
        ),
        name="scatter",
    )(*totals, small)


def local(dp_count, fsdp_count, inputs, lengths, grad_out, *params):
    micro, windows, seq, width = inputs.shape
    count = micro * windows
    wq, wk, wv, wm, we, ws, pos = params[:7]
    bq, bv, bm, eb, bs, g1, s1, g2, s2 = params[7:]
    devices = dp_count * fsdp_count
    counts = (dp_count, fsdp_count // 2)
    rows = wq.shape[0]
    remote_path = fsdp_count % 2 == 0 and rows % 16 == 0 and ws.shape[0] <= LANES and LANES % ws.shape[0] == 0
    me = lax.axis_index("dp") * fsdp_count + lax.axis_index("fsdp")
    vectors = (bq, bv, bm, bs, g1, s1, g2, s2)
    if remote_path:
        lane = lax.broadcasted_iota(jnp.int32, (1, LANES), 1)
        per_row, per_row_ff = LANES // rows, LANES // eb.shape[0]
        eight = jnp.where(
            lane // rows == me % per_row, jnp.tile(jnp.stack(vectors), (1, per_row)), jnp.zeros((), BF)
        )
        one = jnp.where(
            lane // eb.shape[0] == me % per_row_ff, jnp.tile(eb[None], (1, per_row_ff)), jnp.zeros((), BF)
        )
        small = jnp.concatenate([eight, one, jnp.zeros((7, LANES), BF)], axis=0)
        gathered = gather_all(counts, (pos.T, wq, wk, wv, small, wm, we, ws))
        post, wq, wk, wv, small, wm, we, ws = gathered
        pos = post.T
        blocks = small.reshape(devices, 16, LANES).astype(F32)
        vec = blocks[:, :8].reshape(devices // per_row, per_row, 8, LANES).sum(1)
        vec = vec.transpose(1, 0, 2).reshape(8, width)
        eb_all = blocks[:, 8].reshape(devices // per_row_ff, per_row_ff, LANES).sum(1).reshape(1, -1)
    else:
        whole = lambda a, axis=0: lax.all_gather(a, AXES, axis=axis, tiled=True)
        wq, wk, wv, wm, we, ws = (whole(a) for a in (wq, wk, wv, wm, we, ws))
        pos = whole(pos, 1)
        vec = jnp.stack([whole(a).astype(F32) for a in vectors])
        eb_all = whole(eb).astype(F32)[None]
    flat = lambda a: a.reshape((count,) + a.shape[2:])
    out, gin, gwq, gwk, gwv, gwm, gwe, gws, gpos, gvec, geb = compute(
        lengths.reshape(count), flat(inputs), flat(grad_out), wq, wk, wv, wm, we, ws, pos, vec, eb_all
    )
    if remote_path:
        small = jnp.concatenate([gvec, geb.reshape(-1, width), jnp.zeros((4, width), F32)], axis=0)
        gwe, gws, gwm, gwq, gwk, gwv, gpost, small = scatter_all(
            counts, (gwe, gws, gwm, gwq, gwk, gwv, gpos.T), small
        )
        gpos = gpost.T
        mine = lax.dynamic_slice(small[:8], (0, me * rows), (8, rows))
        geb = lax.dynamic_slice(small[8:12].reshape(-1), (me * eb.shape[0],), eb.shape)
        gvec = tuple(mine[i] for i in range(8))
    else:
        share = lambda a, axis=0: lax.psum_scatter(a, AXES, scatter_dimension=axis, tiled=True)
        gwq, gwk, gwv, gwm, gwe, gws = (share(a) for a in (gwq, gwk, gwv, gwm, gwe, gws))
        gpos = share(gpos, 1)
        gvec = tuple(share(gvec[i]) for i in range(8))
        geb = share(geb[0])
    gbq, gbv, gbm, gbs, gg1, gs1, gg2, gs2 = gvec
    return (
        out.reshape(inputs.shape), gin.reshape(inputs.shape), gwq, gwk, gwv, gwm, gwe, gws, gpos,
        gbq, gbv, gbm, geb, gbs, gg1, gs1, gg2, gs2,
    )


def solution(mesh):
    batch = P(None, AXES, None, None)
    matrix, vector, table = P(AXES, None), P(AXES), P(None, AXES)
    weights = (matrix,) * 6 + (table,) + (vector,) * 9
    return jax.shard_map(
        functools.partial(local, mesh.shape["dp"], mesh.shape["fsdp"]),
        mesh=mesh,
        in_specs=(batch, P(None, AXES), batch) + weights,
        out_specs=(batch, batch) + weights,
        check_vma=False,
    )
```

time: 1410 us -> 234 us (0.17)
  waiting for transfers between devices: 793 us -> 0 us
  blocking collectives: 285 us -> 0 us
  Pallas kernels: 0 us -> 205 us
  matrix products: 195 us -> 0 us
  other arithmetic: 67.2 us -> 5.62 us
  local copies, waits for them, and re-layouts: 40.4 us -> 20.9 us
  between operations: 15.8 us -> 0.75 us
    reduce_scatter x7 -> x0, waiting for transfers between devices: 792 us -> none  [the longest x1 142 us: local(): lax.psum_scatter(accumulated[5], ('dp', 'fsdp'), scatter_dimension=0, til...]
    pallas_call x0 -> x3, Pallas kernels: none -> 205 us  [the longest x1 94.7 us: compute(): pl.pallas_call(functools.partial(compute_kernel, names, phases), out_shap...]
    all_gather x5 -> x0, blocking collectives: 204 us -> none  [the longest x1 43.1 us: local(): lax.all_gather(query_weight, ('dp', 'fsdp'), axis=0, tiled=True)]
    dot_general x48 -> x0, matrix products: 195 us -> none  [the longest x12 41.4 us: project_back(): jnp.einsum('wse,de->wsd', gradient, weight, preferred_element_type=jnp.fl...]
    unnamed x2 -> x0, blocking collectives: 81 us -> none
    reduce_sum x11 -> x2, other arithmetic: 34.1 us -> 1.24 us  [the longest x1 0.62 us: local(): blocks[:, 8].reshape(devices // per_row_ff, per_row_ff, LANES).sum(1)]
    unnamed x253 -> x9, local copies, waits for them, and re-layouts: 37.6 us -> 10.7 us
    convert_element_type x14 -> x1, other arithmetic: 26.1 us -> 0.92 us  [local(): blocks = small.reshape(devices, 16, LANES).astype(F32)]
  transfers between devices with their start and end apart: 9 -> 0, of which waited for: 6 -> 0; matrix products, arithmetic and copies ran while one was open for 15% -> 0% of each run, Pallas kernels for 0% -> 0%
where the time goes in v1:
time: 234 us; the launch traced here: 233 us
  Pallas kernels  205 us (88%)
  local copies, waits for them, and re-layouts  20.9 us (9%)
  other arithmetic  5.62 us (2%)
    pallas_call x1, Pallas kernels, compute(): pl.pallas_call(functools.partial(compute_kernel, names, phases), out_shap...  94.7 us
    pallas_call x1, Pallas kernels, scatter_all(): pl.pallas_call(functools.partial(scatter_kernel, counts, len(totals)), ou...  57.1 us
    pallas_call x1, Pallas kernels, gather_all(): pl.pallas_call(functools.partial(gather_kernel, counts, len(shards)), out...  53.7 us
    unnamed x9, local copies, waits for them, and re-layouts  10.7 us

profile of v1, /device:TPU:0, one launch (start us, length us, event | category | flops | bytes accessed | tf_op | source)
XLA Modules:
  0.0 232.7 jit_solution(8142400432950892856)
XLA Ops:
  0.7 0.8 stack.35
  1.5 0.1 tile.18
  1.6 0.7 tile.19
  2.3 0.1 tile.20
  2.4 0.1 pad.5.clone
  2.4 0.7 maximum_maximum_fusion.1.refs_4_
  3.1 53.7 %gather.1 = (bf16[4,4,2,16,512]{4,3,2,1,0:T(8,128)(2,1)}, bf16[4,4,2,16,512]{4,3,2,1,0:T(8,128)(2,1)}, bf16[4,4,2,16,512]{4,3,2,1,0:T(8,128)(2,1)}, bf16[4,4,2,1...) custom-call(bf16[16,512]{1,0:T(8,128)(2,1)} %bitcast.81, ...), custom_call_target="tpu_custom_call" | custom-call | tf_op jit(solution)/shard_map/gather/pallas_call | solution.py:519
  56.8 2.0 copy.39
  58.9 0.9 bitcast_convert_fusion
  59.8 0.6 reduce_sum.19
  60.4 0.6 bitcast_reduce_fusion
  61.1 1.3 reshape.228.refs_0_
  62.3 94.7 %layer.1 = (bf16[4,512,512]{2,1,0:T(8,128)(2,1)}, bf16[4,512,512]{2,1,0:T(8,128)(2,1)}, f32[512,512]{1,0:T(8,128)}, f32[512,512]{1,0:T(8,128)}, f32[512,512]{1,0...) custom-call(s32[4]{0:T(128)} %reshape.228.refs_0_, ...), custom_call_target="tpu_custom_call" | custom-call | tf_op jit(solution)/shard_map/layer/pallas_call | solution.py:287
  157.0 0.5 broadcast.123
  157.5 1.4 reduce.3
  158.9 0.1 pad.2.clone
  159.0 1.4 maximum_maximum_fusion.refs_7_
  160.4 2.6 %copy.40 = f32[512,512]{1,0:T(8,128)} copy(f32[512,512]{0,1:T(8,128)} %bitcast.67) | data formatting | bytes 2097152 | tf_op jit(solution)/shard_map/transpose | solution.py:636
  163.0 57.1 %scatter.1 = (f32[16,2048]{1,0:T(8,128)}, f32[64,512]{1,0:T(8,128)}, f32[16,512]{1,0:T(8,128)}, f32[16,512]{1,0:T(8,128)}, f32[16,512]{1,0:T(8,128)}, /*index=5*...) custom-call(f32[4,4,2,16,2048]{4,3,2,1,0:T(8,128)} %bitcast.59, f32[4,4,2,64,512]{4,3,2,1,0:T(8,128)} %bitcast.60, ...), custom_call_target="tpu_custom_call" | custom-call | tf_op jit(solution)/shard_map/scatter/pallas_call | solution.py:581
  220.1 0.7 slice.38
  220.8 0.1 constant_dynamic-slice_fusion
  220.9 0.5 slice_bitcast_fusion.1
  221.4 0.7 slice_bitcast_fusion
  222.1 0.6 dynamic_slice.7
  222.7 1.4 copy.49
  224.1 1.4 copy.50
  225.5 1.4 copy.51
  226.9 1.4 copy.52
  228.2 1.6 copy.53
  229.8 1.6 copy.54
  231.4 1.4 copy.55
  (9 shorter events, 0.1 us)

commit v2 on v1

v2 whole, which is shorter than its diff:
```python
import functools

import jax
import jax.numpy as jnp
from jax import lax
from jax.experimental import pallas as pl
from jax.experimental.pallas import tpu as pltpu
from jax.sharding import PartitionSpec as P

HEADS = 8
EPS = 1e-05
BF = jnp.bfloat16
F32 = jnp.float32
GELU_C = 0.7978845608028654
GELU_A = 0.044715
AXES = ("dp", "fsdp")
LANES = 128
MESH = pl.DeviceIdType.MESH
FF_PARTS = 2

(BQ, BV, BM, BS, G1, S1, G2, S2) = range(8)


class Refs:
    def __init__(self, **kw):
        self.__dict__.update(kw)


def nn(a, b):
    return lax.dot_general(a, b, (((1,), (0,)), ((), ())), preferred_element_type=F32)


def nt(a, b):
    return lax.dot_general(a, b, (((1,), (1,)), ((), ())), preferred_element_type=F32)


def tn(a, b):
    return lax.dot_general(a, b, (((0,), (0,)), ((), ())), preferred_element_type=F32)


def flat(value):
    return value.reshape(-1, value.shape[-1])


def add_into(ref, value):
    ref[...] += value.reshape(ref.shape)


def add_row(ref, index, value):
    ref[index : index + 1, :] += jnp.sum(value, axis=0, keepdims=True)


def make_mask(w, r):
    seq = r.x.shape[1]
    key_at = lax.broadcasted_iota(jnp.int32, (seq, seq), 0)
    query_at = lax.broadcasted_iota(jnp.int32, (seq, seq), 1)
    ok = (key_at <= query_at) & (key_at < r.lens[w])
    r.mask[...] = jnp.where(ok, 0.0, -1e30)


def hidden_and_keys(w, r):
    low = (r.x[w].astype(F32) + r.pos[...].astype(F32)).astype(BF)
    r.low[w] = low
    r.k[w] = nn(low, flat(r.wk[...])).astype(BF)


def attention_forward(w, r, hook):
    seq, width = r.x.shape[1:]
    half = seq // 2
    head = width // HEADS
    low = r.low[w]
    queries = (nn(low, flat(r.wq[...])) + r.vec[BQ : BQ + 1, :]).astype(BF)
    r.q[w] = (queries.astype(F32) * (head**-0.5)).astype(BF)
    values = (nn(low, flat(r.wv[...])) + r.vec[BV : BV + 1, :]).astype(BF)
    r.v[w] = values
    r.vt[...] = values.T
    make_mask(w, r)
    lane = lax.broadcasted_iota(jnp.int32, (seq, 2 * head), 1)
    for h in range(HEADS):
        if h == HEADS // 2:
            hook(w)
        pair = slice((h // 2) * 2 * head, (h // 2 + 1) * 2 * head)
        mine = (lane < head) if h % 2 == 0 else (lane >= head)
        qh = jnp.where(mine, r.q[w, :, pair], jnp.zeros((), BF))
        kp = r.k[w, :, pair]
        s0 = nt(kp[:half], qh) + r.mask[:half, :]
        s1 = nt(kp[half:], qh[half:]) + r.mask[half:, half:]
        m_left = jnp.max(s0[:, :half], axis=0, keepdims=True)
        m_right = jnp.maximum(
            jnp.max(s0[:, half:], axis=0, keepdims=True), jnp.max(s1, axis=0, keepdims=True)
        )
        top = jnp.concatenate([m_left, m_right], axis=1)
        e0 = jnp.exp(s0 - top)
        e1 = jnp.exp(s1 - m_right)
        n_all = jnp.sum(e0, axis=0, keepdims=True)
        n_right = n_all[:, half:] + jnp.sum(e1, axis=0, keepdims=True)
        total = jnp.concatenate([n_all[:, :half], n_right], axis=1)
        r.logt[w, h : h + 1, :] = top + jnp.log(total)
        inv = 1.0 / total
        p0 = (e0 * inv).astype(BF)
        p1 = (e1 * inv[:, half:]).astype(BF)
        vt = r.vt[h * head : (h + 1) * head, :]
        o_left = nn(vt[:, :half], p0[:, :half])
        o_right = nn(vt, jnp.concatenate([p0[:, half:], p1], axis=0))
        r.ot[h * head : (h + 1) * head, :half] = o_left.astype(BF)
        r.ot[h * head : (h + 1) * head, half:] = o_right.astype(BF)
    r.mixed[w] = r.ot[...].T


def norm_parts(total):
    center = total - jnp.mean(total, -1, keepdims=True)
    spread = jnp.mean(center * center, -1, keepdims=True)
    inv = lax.rsqrt(spread + EPS)
    return center * inv, inv


def norm_back(e, xhat, inv):
    return inv * (
        e - jnp.mean(e, -1, keepdims=True) - xhat * jnp.mean(e * xhat, -1, keepdims=True)
    )


def feed_forward(w, part, r):
    rows, width = r.nl.shape[0] // FF_PARTS, r.x.shape[-1]
    here = pl.ds(pl.multiple_of(part * rows, rows), rows)
    chunks = r.ws.shape[0]
    chunk = r.we.shape[-1] // chunks
    hid = r.x[w, here, :].astype(F32) + r.pos[here, :].astype(F32)
    first = hid + (nn(r.mixed[w, here, :], flat(r.wm[...])) + r.vec[BM : BM + 1, :])
    xhat1, inv1 = norm_parts(first)
    r.xh1[:rows] = xhat1
    normed = xhat1 * r.vec[G1 : G1 + 1, :] + r.vec[S1 : S1 + 1, :]
    r.nl[:rows] = normed.astype(BF)
    ff_out = None
    for c in range(chunks):
        cols = slice(c * chunk, (c + 1) * chunk)
        t = nn(r.nl[:rows], flat(r.we[..., cols])) + r.eb[:, cols]
        t2 = t * t
        th = jnp.tanh(t * (t2 * (GELU_A * GELU_C) + GELU_C))
        ht = 0.5 * t
        act = (ht * th + ht).astype(BF)
        r.act[:, cols] = act
        slope = (0.5 * th + 0.5) + ht * (1.0 - th * th) * (t2 * (3 * GELU_A * GELU_C) + GELU_C)
        r.slope[:, cols] = slope
        part_out = nn(act, flat(r.ws[c]))
        ff_out = part_out if ff_out is None else ff_out + part_out
    second = normed + (ff_out + r.vec[BS : BS + 1, :])
    xhat2, inv2 = norm_parts(second)
    row_at = part * rows + lax.broadcasted_iota(jnp.int32, (rows, width), 0)
    cot = jnp.where(row_at < r.lens[w], r.go[w, here, :].astype(F32), 0.0)
    r.go[w, here, :] = (xhat2 * r.vec[G2 : G2 + 1, :] + r.vec[S2 : S2 + 1, :]).astype(BF)
    add_row(r.gvec, G2, cot * xhat2)
    add_row(r.gvec, S2, cot)
    d_second = norm_back(cot * r.vec[G2 : G2 + 1, :], xhat2, inv2)
    gff = d_second.astype(BF)
    r.gff[:rows] = gff
    add_row(r.gvec, BS, gff.astype(F32))
    d_normed = d_second
    for c in range(chunks):
        cols = slice(c * chunk, (c + 1) * chunk)
        gpre = (nt(r.gff[:rows], flat(r.ws[c])) * r.slope[:, cols]).astype(BF)
        r.geb[:, cols] += jnp.sum(gpre.astype(F32), axis=0, keepdims=True)
        r.gws[c] += tn(r.act[:, cols], r.gff[:rows]).reshape(r.gws.shape[1:])
        r.gwe[..., cols] += tn(r.nl[:rows], gpre).reshape(r.gwe.shape[:-1] + (chunk,))
        d_normed = d_normed + nt(gpre, flat(r.we[..., cols]))
    xhat1 = r.xh1[:rows]
    add_row(r.gvec, G1, d_normed * xhat1)
    add_row(r.gvec, S1, d_normed)
    d_first = norm_back(d_normed * r.vec[G1 : G1 + 1, :], xhat1, inv1)
    r.dfirst[w, here, :] = d_first
    gattn = d_first.astype(BF)
    add_row(r.gvec, BM, gattn.astype(F32))
    mixed = r.mixed[w, here, :]
    add_into(r.gwm, tn(mixed, gattn))
    gmix = nt(gattn, flat(r.wm[...])).astype(BF)
    head = width // HEADS
    prod = gmix.astype(F32) * mixed.astype(F32)
    hi = prod.astype(BF)
    lo = (prod - hi.astype(F32)).astype(BF)
    sel_row = lax.broadcasted_iota(jnp.int32, (16, width), 0)
    sel_col = lax.broadcasted_iota(jnp.int32, (16, width), 1)
    sel = jnp.where(sel_col // head == sel_row, 1.0, 0.0).astype(BF)
    r.delta[w, :, here] = nt(sel, hi) + nt(sel, lo)
    r.mixed[w, here, :] = gmix


def attention_backward(w, r, hook):
    seq, width = r.x.shape[1:]
    half = seq // 2
    head = width // HEADS
    scale = head**-0.5
    make_mask(w, r)
    r.vt[...] = r.k[w].T
    lane = lax.broadcasted_iota(jnp.int32, (seq, 2 * head), 1)
    for p in range(HEADS // 2):
        if p == HEADS // 4:
            hook(w)
        pair = slice(p * 2 * head, (p + 1) * 2 * head)
        kp = r.k[w, :, pair]
        vp = r.v[w, :, pair]
        sums = None
        for odd in range(2):
            h = 2 * p + odd
            mine = (lane >= head) if odd else (lane < head)
            qh = jnp.where(mine, r.q[w, :, pair], jnp.zeros((), BF))
            gh = jnp.where(mine, r.mixed[w, :, pair], jnp.zeros((), BF))
            logt = r.logt[w, h : h + 1, :]
            delta = r.delta[w, h : h + 1, :]
            p0 = jnp.exp(nt(kp[:half], qh) + r.mask[:half, :] - logt)
            p1 = jnp.exp(nt(kp[half:], qh[half:]) + r.mask[half:, half:] - logt[:, half:])
            d0 = (p0 * (nt(vp[:half], gh) - delta)).astype(BF)
            d1 = (p1 * (nt(vp[half:], gh[half:]) - delta[:, half:])).astype(BF)
            p0 = p0.astype(BF)
            p1 = p1.astype(BF)
            parts = (nn(d0, qh), nn(d1, qh[half:]), nn(p0, gh), nn(p1, gh[half:]))
            sums = parts if sums is None else tuple(a + b for a, b in zip(sums, parts))
            kt = r.vt[h * head : (h + 1) * head, :]
            q_left = nn(kt[:, :half], d0[:, :half])
            q_right = nn(kt, jnp.concatenate([d0[:, half:], d1], axis=0))
            r.ot[h * head : (h + 1) * head, :half] = (q_left * scale).astype(BF)
            r.ot[h * head : (h + 1) * head, half:] = (q_right * scale).astype(BF)
        r.nl[:half, pair] = sums[0].astype(BF)
        r.nl[half:, pair] = sums[1].astype(BF)
        r.gff[:half, pair] = sums[2].astype(BF)
        r.gff[half:, pair] = sums[3].astype(BF)
    gq = r.ot[...].T
    gk = r.nl[...]
    gv = r.gff[...]
    low = r.low[w]
    add_into(r.gwq, tn(low, gq))
    add_into(r.gwk, tn(low, gk))
    add_into(r.gwv, tn(low, gv))
    add_row(r.gvec, BQ, gq.astype(F32))
    add_row(r.gvec, BV, gv.astype(F32))
    d_hidden = (
        r.dfirst[w]
        + nt(gq, flat(r.wq[...]))
        + nt(gk, flat(r.wk[...]))
        + nt(gv, flat(r.wv[...]))
    )
    r.gpos[...] += d_hidden
    r.x[w] = d_hidden.astype(BF)


def windows(count, body):
    def step(w, carry):
        body(w)
        return carry

    lax.fori_loop(0, count, step, 0)


def at_window(w, plan):
    for index, steps in plan:

        @pl.when(w == index)
        def _():
            for step in steps:
                step()


class Place:
    def __init__(self, dp_count, z_count):
        self.dp_count, self.z_count = dp_count, z_count
        self.dp = lax.axis_index("dp")
        fsdp = lax.axis_index("fsdp")
        self.z, self.c = fsdp // 2, lax.rem(fsdp, 2)
        self.near = (self.dp, self.z * 2 + (1 - self.c))

    def z_at(self, shift):
        return lax.rem(self.z + shift + self.z_count, self.z_count)

    def dp_flip(self, bit):
        low, high = lax.rem(self.dp, 2), self.dp // 2
        if bit in (0, 2):
            low = 1 - low
        if bit in (1, 2):
            high = 1 - high
        return high * 2 + low

    def along_z(self, shift):
        return (self.dp, self.z_at(shift) * 2 + self.c)

    def along_dp(self, bit):
        return (self.dp_flip(bit), self.z * 2 + self.c)

    def barrier(self):
        sem = pltpu.get_barrier_semaphore()
        everyone = [self.near] + [self.along_z(s) for s in range(1, self.z_count)]
        everyone += [self.along_dp(bit) for bit in range(3)]
        for peer in everyone:
            pl.semaphore_signal(sem, inc=1, device_id=peer, device_id_type=MESH)
        pl.semaphore_wait(sem, len(everyone))


def remote(src, dst, sems, index, peer):
    send, recv = sems
    return pltpu.make_async_remote_copy(
        src_ref=src, dst_ref=dst, send_sem=send.at[index], recv_sem=recv.at[index],
        device_id=peer, device_id_type=MESH,
    )


def hop_count(dp_count, z_count):
    return (z_count - 1) + 3 + 1


class Gather:
    def __init__(self, place, shard, whole, sems, first):
        self.p, self.shard, self.whole, self.sems = place, shard, whole, sems
        self.first, self.second = first, 1 - first
        self.base = place.z_count - 1

    def z_copy(self, shift, z):
        p = self.p
        return remote(self.shard, self.whole.at[p.dp, z, p.c], self.sems, shift - 1, p.along_z(shift))

    def dp_copy(self, slot, owner, bit):
        p = self.p
        block = self.whole.at[owner, :, p.c]
        return remote(block, block, self.sems, self.base + slot, p.along_dp(bit))

    def sent(self):
        p = self.p
        return [
            self.dp_copy(0, p.dp, self.first),
            self.dp_copy(1, p.dp, self.second),
            self.dp_copy(2, p.dp_flip(self.first), self.second),
        ]

    def taken(self):
        p = self.p
        return [
            self.dp_copy(0, p.dp_flip(self.first), self.first),
            self.dp_copy(1, p.dp_flip(self.second), self.second),
            self.dp_copy(2, p.dp_flip(2), self.second),
        ]

    def core_copy(self, core):
        half = self.whole.at[:, :, core]
        return remote(half, half, self.sems, self.base + 3, self.p.near)

    def start_z(self):
        p = self.p
        for shift in range(1, p.z_count):
            self.z_copy(shift, p.z).start()
        self.whole[p.dp, p.z, p.c] = self.shard[...]

    def start_dp(self):
        p = self.p
        for shift in range(1, p.z_count):
            self.z_copy(shift, p.z_at(-shift)).wait_recv()
        sent = self.sent()
        sent[0].start()
        sent[1].start()

    def pass_on(self):
        self.taken()[0].wait_recv()
        self.sent()[2].start()

    def start_core(self):
        taken = self.taken()
        taken[1].wait_recv()
        taken[2].wait_recv()
        self.core_copy(self.p.c).start()

    def finish(self):
        self.core_copy(1 - self.p.c).wait_recv()

    def drain(self):
        p = self.p
        for shift in range(1, p.z_count):
            self.z_copy(shift, p.z).wait_send()
        for copy in self.sent():
            copy.wait_send()
        self.core_copy(p.c).wait_send()


class Scatter:
    def __init__(self, place, total, result, bufs, sems, first):
        self.p, self.total, self.result, self.sems = place, total, result, sems
        self.out, self.from_core, self.from_dp, self.from_z = bufs
        self.first, self.second = first, 1 - first
        self.base = place.z_count - 1

    def core_copy(self):
        return remote(self.out, self.from_core, self.sems, self.base + 3, self.p.near)

    def dp_copies(self):
        p = self.p
        mine, other, far = (p.dp_flip(bit) for bit in (self.first, self.second, 2))
        return [
            remote(self.out.at[far], self.from_dp.at[0], self.sems, self.base, p.along_dp(self.first)),
            remote(self.out.at[mine], self.from_dp.at[1], self.sems, self.base + 1, p.along_dp(self.first)),
            remote(self.out.at[other], self.from_dp.at[2], self.sems, self.base + 2, p.along_dp(self.second)),
        ]

    def z_copy(self, shift):
        p = self.p
        block = self.out.at[p.dp, p.z_at(shift)]
        return remote(block, self.from_z.at[shift - 1], self.sems, shift - 1, p.along_z(shift))

    def blocks(self, body):
        p = self.p

        def step(at, carry):
            body(at // p.z_count, lax.rem(at, p.z_count))
            return carry

        lax.fori_loop(0, p.dp_count * p.z_count, step, 0)

    def start_core(self):
        far = 1 - self.p.c

        def body(d, z):
            self.out[d, z] = self.total[d, z, far].astype(BF)

        self.blocks(body)
        self.core_copy().start()

    def start_dp(self):
        c = self.p.c
        copy = self.core_copy()
        copy.wait_recv()
        copy.wait_send()

        def body(d, z):
            both = self.total[d, z, c] + self.from_core[d, z].astype(F32)
            self.total[d, z, c] = both
            self.out[d, z] = both.astype(BF)

        self.blocks(body)
        copies = self.dp_copies()
        copies[0].start()
        copies[1].start()

    def pass_on(self):
        p = self.p
        copies = self.dp_copies()
        copies[0].wait_recv()
        other = p.dp_flip(self.second)
        for z in range(p.z_count):
            added = self.total[other, z, p.c] + self.from_dp[0, z].astype(F32)
            self.out[other, z] = added.astype(BF)
        copies[2].start()

    def start_z(self):
        p = self.p
        copies = self.dp_copies()
        copies[1].wait_recv()
        copies[2].wait_recv()
        for z in range(p.z_count):
            added = self.total[p.dp, z, p.c] + self.from_dp[1, z].astype(F32) + self.from_dp[2, z].astype(F32)
            self.total[p.dp, z, p.c] = added
            self.out[p.dp, z] = added.astype(BF)
        for shift in range(1, p.z_count):
            self.z_copy(shift).start()

    def finish(self):
        p = self.p
        added = self.total[p.dp, p.z, p.c]
        for shift in range(1, p.z_count):
            self.z_copy(shift).wait_recv()
            added = added + self.from_z[shift - 1].astype(F32)
        self.result[...] = added

    def drain(self):
        for copy in self.dp_copies():
            copy.wait_send()
        for shift in range(1, self.p.z_count):
            self.z_copy(shift).wait_send()


class SumAll:
    def __init__(self, place, total, result, bufs, sems):
        self.p, self.total, self.result, self.sems = place, total, result, sems
        self.send_dp, self.send_z, self.landing = bufs

    def copies(self, hop):
        p = self.p
        base = p.z_count - 1
        if hop == 0:
            return [(base + 3, remote(self.total, self.landing.at[base + 3], self.sems, base + 3, p.near))]
        if hop == 1:
            return [
                (base + b, remote(self.send_dp, self.landing.at[base + b], self.sems, base + b, p.along_dp(b)))
                for b in range(3)
            ]
        return [
            (s - 1, remote(self.send_z, self.landing.at[s - 1], self.sems, s - 1, p.along_z(s)))
            for s in range(1, p.z_count)
        ]

    def arrived(self, hop, own):
        added = own[...]
        for slot, copy in self.copies(hop):
            copy.wait_recv()
            added = added + self.landing[slot]
        return added

    def start(self, hop):
        for _, copy in self.copies(hop):
            copy.start()

    def start_core(self):
        self.start(0)

    def start_dp(self):
        self.send_dp[...] = self.arrived(0, self.total)
        self.start(1)

    def pass_on(self):
        pass

    def start_z(self):
        self.send_z[...] = self.arrived(1, self.send_dp)
        self.start(2)

    def finish(self):
        self.result[...] = self.arrived(2, self.send_z)

    def drain(self):
        for hop in range(3):
            for _, copy in self.copies(hop):
                copy.wait_send()


WEIGHTS = ("wk", "wq", "wv", "wm", "we", "ws")
GRADS = ("gws", "gwe", "gwm", "gwq", "gwk", "gwv")
EARLY = ("post", "small", "wk", "wq", "wv")
LATE = ("wm", "we", "ws")
FIRST = dict(post=0, small=0, wk=1, wq=0, wv=1, wm=0, we=0, ws=1, gws=1, gwe=0, gwm=0, gwq=0, gwk=1, gwv=1, gpost=0)


def work_scratch(count, seq, width, ff):
    vm = pltpu.VMEM
    return dict(
        low=vm((count, seq, width), BF),
        q=vm((count, seq, width), BF),
        k=vm((count, seq, width), BF),
        v=vm((count, seq, width), BF),
        mixed=vm((count, seq, width), BF),
        dfirst=vm((count, seq, width), F32),
        logt=vm((count, HEADS, seq), F32),
        delta=vm((count, 16, seq), F32),
        vt=vm((width, seq), BF),
        ot=vm((width, seq), BF),
        mask=vm((seq, seq), F32),
        xh1=vm((seq // FF_PARTS, width), F32),
        nl=vm((seq, width), BF),
        gff=vm((seq, width), BF),
        act=vm((seq // FF_PARTS, ff), BF),
        slope=vm((seq // FF_PARTS, ff), F32),
        gpos=vm((seq, width), F32),
        x=vm((count, seq, width), BF),
        go=vm((count, seq, width), BF),
        io_sem=pltpu.SemaphoreType.DMA((4, count)),
    )


def zero_sums(r):
    for name in GRADS:
        ref = getattr(r, name)

        def step(at, carry):
            ref[at // ref.shape[1], lax.rem(at, ref.shape[1])] = jnp.zeros(ref.shape[2:], ref.dtype)
            return carry

        lax.fori_loop(0, ref.shape[0] * ref.shape[1], step, 0)
    for name in ("gpos", "gvec", "geb"):
        ref = getattr(r, name)
        ref[...] = jnp.zeros(ref.shape, ref.dtype)


def io_copies(r, count):
    def load(w):
        return (
            pltpu.make_async_copy(r.x_in.at[w], r.x.at[w], r.io_sem.at[0, w]),
            pltpu.make_async_copy(r.go_in.at[w], r.go.at[w], r.io_sem.at[1, w]),
        )

    def store_out(w):
        return pltpu.make_async_copy(r.go.at[w], r.out.at[w], r.io_sem.at[2, w])

    def store_gin(w):
        return pltpu.make_async_copy(r.x.at[w], r.gin.at[w], r.io_sem.at[3, w])

    return load, store_out, store_gin


def alone_kernel(names, *refs):
    r = Refs(**dict(zip(names, refs)))
    count = r.x.shape[0]
    load, store_out, store_gin = io_copies(r, count)
    for w in range(count):
        for copy in load(w):
            copy.start()
    zero_sums(r)
    for w in range(count):
        for copy in load(w):
            copy.wait()

    def second(w):
        windows(FF_PARTS, lambda part: feed_forward(w, part, r))
        store_out(w).start()

    def third(w):
        attention_backward(w, r, lambda w: None)
        store_gin(w).start()

    windows(count, lambda w: hidden_and_keys(w, r))
    windows(count, lambda w: attention_forward(w, r, lambda w: None))
    windows(count, second)
    windows(count, third)
    r.gpos_out[...] = r.gpos[...]
    for w in range(count):
        store_out(w).wait()
        store_gin(w).wait()


def vectors_from(r, dp_count, z_count, rows):
    devices = dp_count * z_count * 2
    per_row = LANES // rows
    ff_rows = r.eb.shape[1] // devices
    per_row_ff = LANES // ff_rows

    def block(d):
        return r.small[d // (2 * z_count), (d // 2) % z_count, d % 2].astype(F32)

    for g in range(devices // per_row):
        added = block(g * per_row)[:8]
        for d in range(g * per_row + 1, (g + 1) * per_row):
            added = added + block(d)[:8]
        r.vec[:, g * LANES : (g + 1) * LANES] = added
    for g in range(devices // per_row_ff):
        added = block(g * per_row_ff)[8:9]
        for d in range(g * per_row_ff + 1, (g + 1) * per_row_ff):
            added = added + block(d)[8:9]
        r.eb[:, g * LANES : (g + 1) * LANES] = added


def place_small(r, place):
    rows, ff_rows = r.eight.shape[1], r.one.shape[1]
    me = (place.dp * place.z_count + place.z) * 2 + place.c

    def spread(n):
        at = lax.rem(me, LANES // n) * n
        source = lax.broadcasted_iota(jnp.int32, (n, LANES), 0)
        target = lax.broadcasted_iota(jnp.int32, (n, LANES), 1)
        return jnp.where(target == source + at, 1.0, 0.0).astype(BF)

    r.small_shard[0:8, :] = nn(r.eight[...], spread(rows))
    r.small_shard[8:16, :] = jnp.broadcast_to(nn(r.one[...], spread(ff_rows))[:1], (8, LANES))


def whole_kernel(counts, names, *refs):
    r = Refs(**dict(zip(names, refs)))
    count = r.x.shape[0]
    rows = r.wq_shard.shape[0]
    place = Place(*counts)
    load, store_out, store_gin = io_copies(r, count)
    for w in range(count):
        for copy in load(w):
            copy.start()
    place_small(r, place)
    r.small_low[...] = r.small_shard[...].astype(BF)
    gathers = {}
    for name in EARLY + LATE:
        shard = r.small_low if name == "small" else getattr(r, name + "_shard")
        sems = (getattr(r, name + "_send"), getattr(r, name + "_recv"))
        gathers[name] = Gather(place, shard, getattr(r, name), sems, FIRST[name])
    early = [gathers[name] for name in EARLY]
    late = [gathers[name] for name in LATE]
    place.barrier()
    for job in early + late:
        job.start_z()
    zero_sums(r)
    for job in early:
        job.start_dp()
    for job in early:
        job.pass_on()
    for job in early:
        job.start_core()
    for job in late:
        job.start_dp()
    for job in early[:3]:
        job.finish()
    r.pos[...] = flat(r.post[...]).T
    vectors_from(r, counts[0], counts[1], rows)
    for w in range(count):
        for copy in load(w):
            copy.wait()
    windows(count, lambda w: hidden_and_keys(w, r))
    for job in early[3:]:
        job.finish()

    wm, we, ws = late
    first_plan = ((1, (wm.pass_on, we.pass_on)), (3, (ws.pass_on, wm.start_core)))
    first_mid = ()

    def first_body(w):
        at_window(w, first_plan)
        attention_forward(w, r, lambda at: at_window(at, first_mid))

    windows(count, first_body)
    we.start_core()
    ws.start_core()
    for job in late:
        job.finish()

    def second_body(w):
        windows(FF_PARTS, lambda part: feed_forward(w, part, r))
        store_out(w).start()

    windows(count, second_body)

    scatters = {}
    for name in GRADS + ("gpost",):
        total = r.gpost_sum if name == "gpost" else getattr(r, name)
        bufs = [getattr(r, name + tail) for tail in ("_out", "_core", "_dp", "_z")]
        sems = (getattr(r, name + "_send"), getattr(r, name + "_recv"))
        scatters[name] = Scatter(place, total, getattr(r, name + "_result"), bufs, sems, FIRST[name])
    sums = SumAll(
        place, r.gsmall, r.gsmall_result, (r.gsmall_dp, r.gsmall_z, r.gsmall_in), (r.gsmall_send, r.gsmall_recv)
    )
    gws, gwe, gwm = (scatters[name] for name in ("gws", "gwe", "gwm"))
    last = [scatters[name] for name in ("gwq", "gwk", "gwv", "gpost")]
    gws.start_core()
    gwe.start_core()
    gwm.start_core()
    third_plan = ((1, (gwe.start_dp, gwm.start_dp)), (3, (gwe.pass_on, gwm.pass_on)))
    third_mid = ((0, (gws.start_dp,)), (2, (gws.pass_on,)), (3, (gws.start_z,)))

    def third_body(w):
        at_window(w, third_plan)
        attention_backward(w, r, lambda at: at_window(at, third_mid))
        store_gin(w).start()

    windows(count, third_body)
    for job in last[:3]:
        job.start_core()
    add_blocks = r.gpos[...].T
    r.gpost_sum[...] = add_blocks.reshape(r.gpost_sum.shape)
    last[3].start_core()
    ff_rows = r.geb.shape[1] // r.gvec.shape[1]
    width = r.gvec.shape[1]
    r.gsmall[0:8, :] = r.gvec[...]
    r.gsmall[8:16, :] = jnp.zeros((8, width), F32)
    for i in range(ff_rows):
        r.gsmall[8 + i : 9 + i, :] = r.geb[:, i * width : (i + 1) * width]
    sums.start_core()
    last = last + [sums]
    for job in last:
        job.start_dp()
    gwe.start_z()
    gwm.start_z()
    for job in last:
        job.pass_on()
    for job in last:
        job.start_z()
    everyone = [gws, gwe, gwm] + last
    for job in everyone:
        job.finish()
    for job in early + late + everyone:
        job.drain()
    for w in range(count):
        store_out(w).wait()
        store_gin(w).wait()


def unpack_kernel(counts, names, *refs):
    r = Refs(**dict(zip(names, refs)))
    copies = [
        pltpu.make_async_copy(getattr(r, name + "_in"), getattr(r, name), r.sem.at[i])
        for i, name in enumerate(("out", "gin"))
    ]
    for copy in copies:
        copy.start()
    for name in GRADS:
        getattr(r, name)[...] = getattr(r, name + "_in")[...]
    r.gpos[...] = r.gpost_in[...].T
    place = Place(*counts)
    me = (place.dp * place.z_count + place.z) * 2 + place.c
    rows, ff_rows = r.gvec.shape[1], r.geb.shape[1]
    width = r.gsmall_in.shape[1]
    turned = pltpu.roll(r.gsmall_in[0:8, :], width - me * rows, axis=1)
    r.gvec[...] = turned[:, :rows]
    start = me * ff_rows
    lines = r.gsmall_in[8:16, :]
    line_at = lax.broadcasted_iota(jnp.int32, (8, width), 0)
    line = jnp.sum(jnp.where(line_at == start // width, lines, 0.0), axis=0, keepdims=True)
    line = jnp.broadcast_to(line, (8, width))
    r.geb[...] = pltpu.roll(line, width - lax.rem(start, width), axis=1)[0:1, :ff_rows]
    for copy in copies:
        copy.wait()


def call(kernel, name, ins, outs, scratch, **params):
    names = tuple(ins) + tuple(outs) + tuple(scratch)
    spec = lambda space: pl.BlockSpec(memory_space=space)
    results = pl.pallas_call(
        functools.partial(kernel, names),
        out_shape=tuple(shape for shape, _ in outs.values()),
        in_specs=[spec(space) for _, space in ins.values()],
        out_specs=tuple(spec(space) for _, space in outs.values()),
        scratch_shapes=list(scratch.values()),
        compiler_params=pltpu.CompilerParams(vmem_limit_bytes=63 * 2**20, **params),
        name=name,
    )(*[value for value, _ in ins.values()])
    return dict(zip(outs, results))


def local(dp_count, fsdp_count, inputs, lengths, grad_out, *params):
    micro, per_micro, seq, width = inputs.shape
    count = micro * per_micro
    wq, wk, wv, wm, we, ws, pos = params[:7]
    bq, bv, bm, eb, bs, g1, s1, g2, s2 = params[7:]
    ff = we.shape[1]
    rows, ff_rows = wq.shape[0], ws.shape[0]
    vectors = (bq, bv, bm, bs, g1, s1, g2, s2)
    vm, hbm = pltpu.VMEM, pl.ANY
    shape_of = jax.ShapeDtypeStruct
    merged = lambda a: a.reshape((count,) + a.shape[2:])
    act = shape_of((count, seq, width), BF)
    data = dict(
        lens=(lengths.reshape(count), pltpu.SMEM), x_in=(merged(inputs), hbm), go_in=(merged(grad_out), hbm)
    )
    scratch = work_scratch(count, seq, width, ff)
    if dp_count == 4 and fsdp_count % 2 == 0 and rows % 16 == 0 and LANES % rows == 0 and LANES % ff_rows == 0:
        counts = (dp_count, fsdp_count // 2)
        lead = (dp_count, fsdp_count // 2, 2)
        shards = dict(wq=wq, wk=wk, wv=wv, wm=wm, we=we, ws=ws, post=pos.T)
        ins = dict(data)
        for name, shard in shards.items():
            ins[name + "_shard"] = (shard, vm)
        ins["eight"] = (jnp.stack(vectors), vm)
        ins["one"] = (jnp.broadcast_to(eb[None], (8, ff_rows)), vm)
        outs = dict(out=(act, hbm), gin=(act, hbm))
        results = dict(gwq=wq, gwk=wk, gwv=wv, gwm=wm, gwe=we, gws=ws, gpost=pos.T)
        for name, like in results.items():
            outs[name + "_result"] = (shape_of(like.shape, F32), vm)
        outs["gsmall_result"] = (shape_of((16, width), F32), vm)
        hops = hop_count(*counts)
        pair = lambda name: {name + tail: pltpu.SemaphoreType.DMA((hops,)) for tail in ("_send", "_recv")}
        for name, shard in shards.items():
            scratch[name] = vm(lead + shard.shape, BF)
            scratch.update(pair(name))
        scratch["small"] = vm(lead + (16, LANES), BF)
        scratch["small_shard"] = vm((16, LANES), F32)
        scratch["small_low"] = vm((16, LANES), BF)
        scratch["pos"] = vm((seq, width), BF)
        scratch["vec"] = vm((8, width), F32)
        scratch["eb"] = vm((1, ff), F32)
        scratch["gvec"] = vm((8, width), F32)
        scratch["geb"] = vm((1, ff), F32)
        scratch.update(pair("small"))
        scratch.update(pair("gsmall"))
        for name, like in results.items():
            scratch["gpost_sum" if name == "gpost" else name] = vm(lead + like.shape, F32)
            scratch[name + "_out"] = vm(lead[:2] + like.shape, BF)
            scratch[name + "_core"] = vm(lead[:2] + like.shape, BF)
            scratch[name + "_dp"] = vm((3,) + lead[1:2] + like.shape, BF)
            scratch[name + "_z"] = vm((lead[1] - 1,) + like.shape, BF)
            scratch.update(pair(name))
        for tail in ("", "_dp", "_z"):
            scratch["gsmall" + tail] = vm((16, width), F32)
        scratch["gsmall_in"] = vm((hops, 16, width), F32)
        got = call(
            functools.partial(whole_kernel, counts), "layer", ins, outs, scratch,
            collective_id=0, has_side_effects=True,
        )
        ins = {}
        for name in ("out", "gin"):
            ins[name + "_in"] = (got[name], hbm)
        for name in GRADS + ("gpost", "gsmall"):
            ins[name + "_in"] = (got[name + "_result"], vm)
        outs = dict(out=(act, hbm), gin=(act, hbm))
        for name in GRADS:
            outs[name] = (shape_of(results[name].shape, F32), vm)
        outs["gpos"] = (shape_of(pos.shape, F32), vm)
        outs["gvec"] = (shape_of((8, rows), F32), vm)
        outs["geb"] = (shape_of((1, ff_rows), F32), vm)
        got = call(
            functools.partial(unpack_kernel, counts), "unpack", ins, outs, dict(sem=pltpu.SemaphoreType.DMA((2,)))
        )
        gvec, geb, gpos = got["gvec"], got["geb"][0], got["gpos"]
        grads = got
    else:
        lead = (4, 4, 2)
        cut = lambda a: a.reshape(lead + (-1, a.shape[-1]))
        gather = lambda a, axis=0: lax.all_gather(a, AXES, axis=axis, tiled=True)
        share = lambda a, axis=0: lax.psum_scatter(a, AXES, scatter_dimension=axis, tiled=True)
        ins = dict(data)
        for name, shard in dict(wq=wq, wk=wk, wv=wv, wm=wm, we=we, ws=ws).items():
            ins[name] = (cut(gather(shard)), vm)
        ins["pos"] = (gather(pos, 1), vm)
        ins["vec"] = (jnp.stack([gather(a).astype(F32) for a in vectors]), vm)
        ins["eb"] = (gather(eb).astype(F32)[None], vm)
        outs = dict(out=(act, hbm), gin=(act, hbm))
        for name in GRADS:
            outs[name] = (shape_of(ins["w" + name[2:]][0].shape, F32), vm)
        outs["gpos_out"] = (shape_of((seq, width), F32), vm)
        outs["gvec"] = (shape_of((8, width), F32), vm)
        outs["geb"] = (shape_of((1, ff), F32), vm)
        got = call(alone_kernel, "layer_alone", ins, outs, scratch)
        grads = {name: share(flat(got[name])) for name in GRADS}
        gpos = share(got["gpos_out"], 1)
        gvec = [share(got["gvec"][i]) for i in range(8)]
        geb = share(got["geb"][0])
    gbq, gbv, gbm, gbs, gg1, gs1, gg2, gs2 = (gvec[i] for i in range(8))
    return (
        got["out"].reshape(inputs.shape), got["gin"].reshape(inputs.shape),
        grads["gwq"], grads["gwk"], grads["gwv"], grads["gwm"], grads["gwe"], grads["gws"], gpos,
        gbq, gbv, gbm, geb, gbs, gg1, gs1, gg2, gs2,
    )


def solution(mesh):
    batch = P(None, AXES, None, None)
    matrix, vector, table = P(AXES, None), P(AXES), P(None, AXES)
    weights = (matrix,) * 6 + (table,) + (vector,) * 9
    return jax.shard_map(
        functools.partial(local, mesh.shape["dp"], mesh.shape["fsdp"]),
        mesh=mesh,
        in_specs=(batch, P(None, AXES), batch) + weights,
        out_specs=(batch, batch) + weights,
        check_vma=False,
    )
```

time: 234 us -> 296 us (1.26)
  Pallas kernels: 205 us -> 288 us
  local copies, waits for them, and re-layouts: 20.9 us -> 7.06 us
  other arithmetic: 5.62 us -> 0 us
    pallas_call x3 -> x2, Pallas kernels: 205 us -> 288 us  [call(): pl.pallas_call(functools.partial(kernel, names), out_shape=tuple((shape f...]
    unnamed x9 -> x1, local copies, waits for them, and re-layouts: 10.7 us -> 1.67 us
where the time goes in v2:
time: 296 us
  Pallas kernels  288 us (97%)
  local copies, waits for them, and re-layouts  7.06 us (2%)
    pallas_call x2, Pallas kernels, call(): pl.pallas_call(functools.partial(kernel, names), out_shape=tuple((shape f...  288 us

profile of v2, /device:TPU:0, one launch (start us, length us, event | category | flops | bytes accessed | tf_op | source)
XLA Modules:
  0.0 295.5 jit_solution(5451531494865514312)
XLA Ops:
  0.7 1.3 reshape.52.refs_0_
  1.9 1.4 stack.35.refs_10_
  3.3 1.2 broadcast_in_dim.2.refs_11_
  4.5 157.7 %layer.1 = (bf16[4,512,512]{2,1,0:T(8,128)(2,1)}, bf16[4,512,512]{2,1,0:T(8,128)(2,1)}, f32[16,512]{1,0:T(8,128)}, f32[16,512]{1,0:T(8,128)}, f32[16,512]{1,0:T(...) custom-call(s32[4]{0:T(128)} %reshape.52.refs_0_, ...), custom_call_target="tpu_custom_call" | custom-call | tf_op jit(solution)/shard_map/layer/pallas_call | solution.py:801
  162.2 130.1 %unpack.1 = (bf16[4,512,512]{2,1,0:T(8,128)(2,1)}, bf16[4,512,512]{2,1,0:T(8,128)(2,1)}, f32[64,512]{1,0:T(8,128)}, f32[16,2048]{1,0:T(8,128)}, f32[16,512]{1,0:...) custom-call(bf16[4,512,512]{2,1,0:T(8,128)(2,1)} %get-tuple-element., ...), custom_call_target="tpu_custom_call" | custom-call | tf_op jit(solution)/shard_map/unpack/pallas_call | solution.py:801
  292.3 1.5 slice_bitcast_fusion
  293.8 1.7 copy.37

commit v3 on v2

--- a/solution.py
+++ b/solution.py
@@ -50,11 +50,16 @@
     ref[index : index + 1, :] += jnp.sum(value, axis=0, keepdims=True)
 
 
+def length_of(w, r):
+    per_micro = r.lens.shape[1]
+    return r.lens[w // per_micro, lax.rem(w, per_micro)]
+
+
 def make_mask(w, r):
     seq = r.x.shape[1]
     key_at = lax.broadcasted_iota(jnp.int32, (seq, seq), 0)
     query_at = lax.broadcasted_iota(jnp.int32, (seq, seq), 1)
-    ok = (key_at <= query_at) & (key_at < r.lens[w])
+    ok = (key_at <= query_at) & (key_at < length_of(w, r))
     r.mask[...] = jnp.where(ok, 0.0, -1e30)
 
 
@@ -147,7 +152,7 @@
     second = normed + (ff_out + r.vec[BS : BS + 1, :])
     xhat2, inv2 = norm_parts(second)
     row_at = part * rows + lax.broadcasted_iota(jnp.int32, (rows, width), 0)
-    cot = jnp.where(row_at < r.lens[w], r.go[w, here, :].astype(F32), 0.0)
+    cot = jnp.where(row_at < length_of(w, r), r.go[w, here, :].astype(F32), 0.0)
     r.go[w, here, :] = (xhat2 * r.vec[G2 : G2 + 1, :] + r.vec[S2 : S2 + 1, :]).astype(BF)
     add_row(r.gvec, G2, cot * xhat2)
     add_row(r.gvec, S2, cot)
@@ -640,7 +645,7 @@
 
 
 def place_small(r, place):
-    rows, ff_rows = r.eight.shape[1], r.one.shape[1]
+    rows, ff_rows = r.vec0.shape[1], r.ebs.shape[1]
     me = (place.dp * place.z_count + place.z) * 2 + place.c
 
     def spread(n):
@@ -649,8 +654,11 @@
         target = lax.broadcasted_iota(jnp.int32, (n, LANES), 1)
         return jnp.where(target == source + at, 1.0, 0.0).astype(BF)
 
-    r.small_shard[0:8, :] = nn(r.eight[...], spread(rows))
-    r.small_shard[8:16, :] = jnp.broadcast_to(nn(r.one[...], spread(ff_rows))[:1], (8, LANES))
+    for i in range(8):
+        r.eight[i : i + 1, :] = getattr(r, "vec" + str(i))[...].astype(F32)
+    r.small_low[0:8, :] = nn(r.eight[...].astype(BF), spread(rows)).astype(BF)
+    one = jnp.broadcast_to(r.ebs[...].astype(F32), (8, ff_rows)).astype(BF)
+    r.small_low[8:16, :] = nn(one, spread(ff_rows)).astype(BF)
 
 
 def whole_kernel(counts, names, *refs):
@@ -663,7 +671,6 @@
         for copy in load(w):
             copy.start()
     place_small(r, place)
-    r.small_low[...] = r.small_shard[...].astype(BF)
     gathers = {}
     for name in EARLY + LATE:
         shard = r.small_low if name == "small" else getattr(r, name + "_shard")
@@ -770,12 +777,18 @@
 
 def unpack_kernel(counts, names, *refs):
     r = Refs(**dict(zip(names, refs)))
-    copies = [
-        pltpu.make_async_copy(getattr(r, name + "_in"), getattr(r, name), r.sem.at[i])
-        for i, name in enumerate(("out", "gin"))
-    ]
-    for copy in copies:
+    count = r.out.shape[0]
+    loads, stores = [], []
+    for w in range(count):
+        for i, name in enumerate(("out", "gin")):
+            source, target = getattr(r, name + "_in").at[w], getattr(r, name).at[w]
+            loads.append(pltpu.make_async_copy(source, r.held.at[i, w], r.sem.at[0, i, w]))
+            stores.append(pltpu.make_async_copy(r.held.at[i, w], target, r.sem.at[1, i, w]))
+    for copy in loads:
         copy.start()
+    for load, store in zip(loads, stores):
+        load.wait()
+        store.start()
     for name in GRADS:
         getattr(r, name)[...] = getattr(r, name + "_in")[...]
     r.gpos[...] = r.gpost_in[...].T
@@ -791,7 +804,7 @@
     line = jnp.sum(jnp.where(line_at == start // width, lines, 0.0), axis=0, keepdims=True)
     line = jnp.broadcast_to(line, (8, width))
     r.geb[...] = pltpu.roll(line, width - lax.rem(start, width), axis=1)[0:1, :ff_rows]
-    for copy in copies:
+    for copy in stores:
         copy.wait()
 
 
@@ -823,7 +836,7 @@
     merged = lambda a: a.reshape((count,) + a.shape[2:])
     act = shape_of((count, seq, width), BF)
     data = dict(
-        lens=(lengths.reshape(count), pltpu.SMEM), x_in=(merged(inputs), hbm), go_in=(merged(grad_out), hbm)
+        lens=(lengths, pltpu.SMEM), x_in=(merged(inputs), hbm), go_in=(merged(grad_out), hbm)
     )
     scratch = work_scratch(count, seq, width, ff)
     if dp_count == 4 and fsdp_count % 2 == 0 and rows % 16 == 0 and LANES % rows == 0 and LANES % ff_rows == 0:
@@ -833,8 +846,9 @@
         ins = dict(data)
         for name, shard in shards.items():
             ins[name + "_shard"] = (shard, vm)
-        ins["eight"] = (jnp.stack(vectors), vm)
-        ins["one"] = (jnp.broadcast_to(eb[None], (8, ff_rows)), vm)
+        for i, vector in enumerate(vectors):
+            ins["vec" + str(i)] = (vector[None], vm)
+        ins["ebs"] = (eb[None], vm)
         outs = dict(out=(act, hbm), gin=(act, hbm))
         results = dict(gwq=wq, gwk=wk, gwv=wv, gwm=wm, gwe=we, gws=ws, gpost=pos.T)
         for name, like in results.items():
@@ -846,7 +860,7 @@
             scratch[name] = vm(lead + shard.shape, BF)
             scratch.update(pair(name))
         scratch["small"] = vm(lead + (16, LANES), BF)
-        scratch["small_shard"] = vm((16, LANES), F32)
+        scratch["eight"] = vm((8, rows), F32)
         scratch["small_low"] = vm((16, LANES), BF)
         scratch["pos"] = vm((seq, width), BF)
         scratch["vec"] = vm((8, width), F32)
@@ -881,7 +895,8 @@
         outs["gvec"] = (shape_of((8, rows), F32), vm)
         outs["geb"] = (shape_of((1, ff_rows), F32), vm)
         got = call(
-            functools.partial(unpack_kernel, counts), "unpack", ins, outs, dict(sem=pltpu.SemaphoreType.DMA((2,)))
+            functools.partial(unpack_kernel, counts), "unpack", ins, outs,
+            dict(held=vm((2,) + act.shape, BF), sem=pltpu.SemaphoreType.DMA((2, 2, count))),
         )
         gvec, geb, gpos = got["gvec"], got["geb"][0], got["gpos"]
         grads = got

time: 296 us -> 168 us (0.57)
  Pallas kernels: 288 us -> 163 us
  local copies, waits for them, and re-layouts: 7.06 us -> 3.19 us
    pallas_call x2, Pallas kernels: 288 us -> 163 us  [call(): pl.pallas_call(functools.partial(kernel, names), out_shape=tuple((shape f...]
where the time goes in v3:
time: 168 us; the launch traced here: 167 us
  Pallas kernels  163 us (97%)
  local copies, waits for them, and re-layouts  3.19 us (2%)
    pallas_call x2, Pallas kernels, call(): pl.pallas_call(functools.partial(kernel, names), out_shape=tuple((shape f...  163 us

profile of v3, /device:TPU:0, one launch (start us, length us, event | category | flops | bytes accessed | tf_op | source)
XLA Modules:
  0.0 167.4 jit_solution(2966642735865400026)
XLA Ops:
  0.7 158.0 %layer.1 = (bf16[4,512,512]{2,1,0:T(8,128)(2,1)}, bf16[4,512,512]{2,1,0:T(8,128)(2,1)}, f32[16,512]{1,0:T(8,128)}, f32[16,512]{1,0:T(8,128)}, f32[16,512]{1,0:T(...) custom-call(s32[2,2]{1,0:T(2,128)} %refs_0_.1, ...), custom_call_target="tpu_custom_call" | custom-call | tf_op jit(solution)/shard_map/layer/pallas_call | solution.py:814
  158.7 5.5 %unpack.1 = (bf16[4,512,512]{2,1,0:T(8,128)(2,1)}, bf16[4,512,512]{2,1,0:T(8,128)(2,1)}, f32[64,512]{1,0:T(8,128)}, f32[16,2048]{1,0:T(8,128)}, f32[16,512]{1,0:...) custom-call(bf16[4,512,512]{2,1,0:T(8,128)(2,1)} %get-tuple-element., ...), custom_call_target="tpu_custom_call" | custom-call | tf_op jit(solution)/shard_map/unpack/pallas_call | solution.py:814
  164.2 1.5 slice_bitcast_fusion
  165.7 1.7 copy.37

commit v4 on v3

--- a/solution.py
+++ b/solution.py
@@ -16,9 +16,11 @@
 AXES = ("dp", "fsdp")
 LANES = 128
 MESH = pl.DeviceIdType.MESH
-FF_PARTS = 2
+FF_PARTS = 1
+GROUPS = 2
 
 (BQ, BV, BM, BS, G1, S1, G2, S2) = range(8)
+(Q, K, V, LOW) = range(4)
 
 
 class Refs:
@@ -65,29 +67,27 @@
 
 def hidden_and_keys(w, r):
     low = (r.x[w].astype(F32) + r.pos[...].astype(F32)).astype(BF)
-    r.low[w] = low
-    r.k[w] = nn(low, flat(r.wk[...])).astype(BF)
-
-
-def attention_forward(w, r, hook):
+    r.ab[LOW, w] = low
+    r.ab[K, w] = nn(low, flat(r.wk[...])).astype(BF)
+
+
+def attention_forward(w, r):
     seq, width = r.x.shape[1:]
     half = seq // 2
     head = width // HEADS
-    low = r.low[w]
+    low = r.ab[LOW, w]
     queries = (nn(low, flat(r.wq[...])) + r.vec[BQ : BQ + 1, :]).astype(BF)
-    r.q[w] = (queries.astype(F32) * (head**-0.5)).astype(BF)
+    r.ab[Q, w] = (queries.astype(F32) * (head**-0.5)).astype(BF)
     values = (nn(low, flat(r.wv[...])) + r.vec[BV : BV + 1, :]).astype(BF)
-    r.v[w] = values
+    r.ab[V, w] = values
     r.vt[...] = values.T
     make_mask(w, r)
     lane = lax.broadcasted_iota(jnp.int32, (seq, 2 * head), 1)
     for h in range(HEADS):
-        if h == HEADS // 2:
-            hook(w)
         pair = slice((h // 2) * 2 * head, (h // 2 + 1) * 2 * head)
         mine = (lane < head) if h % 2 == 0 else (lane >= head)
-        qh = jnp.where(mine, r.q[w, :, pair], jnp.zeros((), BF))
-        kp = r.k[w, :, pair]
+        qh = jnp.where(mine, r.ab[Q, w, :, pair], jnp.zeros((), BF))
+        kp = r.ab[K, w, :, pair]
         s0 = nt(kp[:half], qh) + r.mask[:half, :]
         s1 = nt(kp[half:], qh[half:]) + r.mask[half:, half:]
         m_left = jnp.max(s0[:, :half], axis=0, keepdims=True)
@@ -110,6 +110,8 @@
         r.ot[h * head : (h + 1) * head, :half] = o_left.astype(BF)
         r.ot[h * head : (h + 1) * head, half:] = o_right.astype(BF)
     r.mixed[w] = r.ot[...].T
+    for i in range(4):
+        park_copy(r, i, w).start()
 
 
 def norm_parts(total):
@@ -125,26 +127,86 @@
     )
 
 
+def slot_of(kind, w, c):
+    return (kind + 2 * lax.rem(w, 2), c)
+
+
+def part_copy(r, kind, w, part, c, rows):
+    here = slice(part * rows, (part + 1) * rows)
+    target = r.kept.at[1 + kind, c, w]
+    return pltpu.make_async_copy(r.ab.at[slot_of(kind, w, c)], target, r.part_sem.at[kind, lax.rem(w, 2), c])
+
+
+def park_copy(r, i, w):
+    return pltpu.make_async_copy(r.ab.at[i, w], r.kept.at[0, i, w], r.park_sem.at[i, w])
+
+
+def finish_parking(r):
+    for i in range(4):
+        for w in range(r.x.shape[0]):
+            park_copy(r, i, w).wait()
+
+
+def block_load(r, kind, c, buffer):
+    return pltpu.make_async_copy(r.kept.at[kind, c], r.ab.at[buffer], r.load_sem.at[buffer])
+
+
+BUFFERS = (2, 3, 0, 1, 2, 0, 1, 3)
+FOLLOWS = {0: (2, 0), 1: (2, 3), 2: (2, 1), 3: (2, 2), 4: (0, 2), 5: (0, 0), 6: (0, 1), 7: (0, 3)}
+
+
+def weight_sums(r, emit, after):
+    count = r.x.shape[0]
+    rows, chunks = r.slope.shape[0], r.ws.shape[0]
+    for kind in range(2):
+        for part in range(FF_PARTS):
+            for c in range(chunks):
+                part_copy(r, kind, count - 2, part, c, rows).wait()
+                part_copy(r, kind, count - 1, part, c, rows).wait()
+    for item in range(4):
+        block_load(r, 1, item, BUFFERS[item]).start()
+    for item in range(2 * chunks):
+        buffer, c = BUFFERS[item], item % chunks
+        block_load(r, 1 + item // chunks, c, buffer).wait()
+        block = flat(r.ab[buffer])
+        if item < chunks:
+            emit(item, tn(block, flat(r.gff[...])))
+        else:
+            emit(item, tn(flat(r.nl[...]), block))
+        block_load(r, *FOLLOWS[item], buffer).start()
+        after(item)
+    for buffer in range(4):
+        block_load(r, 0, buffer, buffer).wait()
+
+
 def feed_forward(w, part, r):
-    rows, width = r.nl.shape[0] // FF_PARTS, r.x.shape[-1]
-    here = pl.ds(pl.multiple_of(part * rows, rows), rows)
+    rows, width = r.slope.shape[0], r.x.shape[-1]
+    here = slice(part * rows, (part + 1) * rows)
     chunks = r.ws.shape[0]
     chunk = r.we.shape[-1] // chunks
+
+    @pl.when(w > 1)
+    def _():
+        for kind in range(2):
+            for c in range(chunks):
+                part_copy(r, kind, w - 2, part, c, rows).wait()
+
     hid = r.x[w, here, :].astype(F32) + r.pos[here, :].astype(F32)
     first = hid + (nn(r.mixed[w, here, :], flat(r.wm[...])) + r.vec[BM : BM + 1, :])
     xhat1, inv1 = norm_parts(first)
-    r.xh1[:rows] = xhat1
+    r.xh1[...] = xhat1
     normed = xhat1 * r.vec[G1 : G1 + 1, :] + r.vec[S1 : S1 + 1, :]
-    r.nl[:rows] = normed.astype(BF)
+    r.nl[w, here, :] = normed.astype(BF)
     ff_out = None
     for c in range(chunks):
         cols = slice(c * chunk, (c + 1) * chunk)
-        t = nn(r.nl[:rows], flat(r.we[..., cols])) + r.eb[:, cols]
+        t = nn(r.nl[w, here, :], flat(r.we[..., cols])) + r.eb[:, cols]
         t2 = t * t
         th = jnp.tanh(t * (t2 * (GELU_A * GELU_C) + GELU_C))
         ht = 0.5 * t
         act = (ht * th + ht).astype(BF)
-        r.act[:, cols] = act
+        slot = slot_of(0, w, c)
+        r.ab[slot] = act
         slope = (0.5 * th + 0.5) + ht * (1.0 - th * th) * (t2 * (3 * GELU_A * GELU_C) + GELU_C)
         r.slope[:, cols] = slope
         part_out = nn(act, flat(r.ws[c]))
@@ -158,17 +220,17 @@
     add_row(r.gvec, S2, cot)
     d_second = norm_back(cot * r.vec[G2 : G2 + 1, :], xhat2, inv2)
     gff = d_second.astype(BF)
-    r.gff[:rows] = gff
+    r.gff[w, here, :] = gff
     add_row(r.gvec, BS, gff.astype(F32))
     d_normed = d_second
     for c in range(chunks):
         cols = slice(c * chunk, (c + 1) * chunk)
-        gpre = (nt(r.gff[:rows], flat(r.ws[c])) * r.slope[:, cols]).astype(BF)
+        gpre = (nt(r.gff[w, here, :], flat(r.ws[c])) * r.slope[:, cols]).astype(BF)
         r.geb[:, cols] += jnp.sum(gpre.astype(F32), axis=0, keepdims=True)
-        r.gws[c] += tn(r.act[:, cols], r.gff[:rows]).reshape(r.gws.shape[1:])
-        r.gwe[..., cols] += tn(r.nl[:rows], gpre).reshape(r.gwe.shape[:-1] + (chunk,))
+        slot = slot_of(1, w, c)
+        r.ab[slot] = gpre
         d_normed = d_normed + nt(gpre, flat(r.we[..., cols]))
-    xhat1 = r.xh1[:rows]
+    xhat1 = r.xh1[...]
     add_row(r.gvec, G1, d_normed * xhat1)
     add_row(r.gvec, S1, d_normed)
     d_first = norm_back(d_normed * r.vec[G1 : G1 + 1, :], xhat1, inv1)
@@ -187,27 +249,30 @@
     sel = jnp.where(sel_col // head == sel_row, 1.0, 0.0).astype(BF)
     r.delta[w, :, here] = nt(sel, hi) + nt(sel, lo)
     r.mixed[w, here, :] = gmix
-
-
-def attention_backward(w, r, hook):
+    for kind in range(2):
+        for c in range(chunks):
+            part_copy(r, kind, w, part, c, rows).start()
+
+
+def attention_backward(w, group, r):
     seq, width = r.x.shape[1:]
     half = seq // 2
     head = width // HEADS
     scale = head**-0.5
+    cols = slice(group * (width // GROUPS), (group + 1) * (width // GROUPS))
     make_mask(w, r)
-    r.vt[...] = r.k[w].T
+    r.vt[cols, :] = r.ab[K, w, :, cols].T
     lane = lax.broadcasted_iota(jnp.int32, (seq, 2 * head), 1)
-    for p in range(HEADS // 2):
-        if p == HEADS // 4:
-            hook(w)
+    pairs = HEADS // 2 // GROUPS
+    for p in range(group * pairs, (group + 1) * pairs):
         pair = slice(p * 2 * head, (p + 1) * 2 * head)
-        kp = r.k[w, :, pair]
-        vp = r.v[w, :, pair]
+        kp = r.ab[K, w, :, pair]
+        vp = r.ab[V, w, :, pair]
         sums = None
         for odd in range(2):
             h = 2 * p + odd
             mine = (lane >= head) if odd else (lane < head)
-            qh = jnp.where(mine, r.q[w, :, pair], jnp.zeros((), BF))
+            qh = jnp.where(mine, r.ab[Q, w, :, pair], jnp.zeros((), BF))
             gh = jnp.where(mine, r.mixed[w, :, pair], jnp.zeros((), BF))
             logt = r.logt[w, h : h + 1, :]
             delta = r.delta[w, h : h + 1, :]
@@ -224,24 +289,33 @@
             q_right = nn(kt, jnp.concatenate([d0[:, half:], d1], axis=0))
             r.ot[h * head : (h + 1) * head, :half] = (q_left * scale).astype(BF)
             r.ot[h * head : (h + 1) * head, half:] = (q_right * scale).astype(BF)
-        r.nl[:half, pair] = sums[0].astype(BF)
-        r.nl[half:, pair] = sums[1].astype(BF)
-        r.gff[:half, pair] = sums[2].astype(BF)
-        r.gff[half:, pair] = sums[3].astype(BF)
-    gq = r.ot[...].T
-    gk = r.nl[...]
-    gv = r.gff[...]
-    low = r.low[w]
-    add_into(r.gwq, tn(low, gq))
-    add_into(r.gwk, tn(low, gk))
-    add_into(r.gwv, tn(low, gv))
-    add_row(r.gvec, BQ, gq.astype(F32))
-    add_row(r.gvec, BV, gv.astype(F32))
+        grads = [part.astype(BF) for part in sums]
+        r.ab[K, w, :half, pair] = grads[0]
+        r.ab[K, w, half:, pair] = grads[1]
+        r.ab[V, w, :half, pair] = grads[2]
+        r.ab[V, w, half:, pair] = grads[3]
+        gq = r.ot[pair, :].T
+        r.ab[Q, w, :, pair] = gq
+        r.gvec[BQ : BQ + 1, pair] += jnp.sum(gq.astype(F32), axis=0, keepdims=True)
+        gv = grads[2].astype(F32) + grads[3].astype(F32)
+        r.gvec[BV : BV + 1, pair] += jnp.sum(gv, axis=0, keepdims=True)
+
+
+def projection_sums(group, r):
+    width = r.x.shape[-1]
+    size = width // GROUPS
+    cols = slice(group * size, (group + 1) * size)
+    total = getattr(r, "gqkv" + str(group))
+    for at, kind in enumerate((Q, K, V)):
+        total[:, at * size : (at + 1) * size] = tn(flat(r.ab[LOW]), flat(r.ab[kind, :, :, cols]))
+
+
+def hidden_back(w, r):
     d_hidden = (
         r.dfirst[w]
-        + nt(gq, flat(r.wq[...]))
-        + nt(gk, flat(r.wk[...]))
-        + nt(gv, flat(r.wv[...]))
+        + nt(r.ab[Q, w], flat(r.wq[...]))
+        + nt(r.ab[K, w], flat(r.wk[...]))
+        + nt(r.ab[V, w], flat(r.wv[...]))
     )
     r.gpos[...] += d_hidden
     r.x[w] = d_hidden.astype(BF)
@@ -307,43 +381,36 @@
 
 
 def hop_count(dp_count, z_count):
-    return (z_count - 1) + 3 + 1
+    return (z_count - 1) + 7
+
+
+def halves(ref):
+    lanes = ref.shape[-1]
+    if lanes % (2 * LANES):
+        return ((0, slice(0, lanes)),)
+    return ((0, slice(0, lanes // 2)), (1, slice(lanes // 2, lanes)))
 
 
 class Gather:
-    def __init__(self, place, shard, whole, sems, first):
+    def __init__(self, place, shard, whole, sems):
         self.p, self.shard, self.whole, self.sems = place, shard, whole, sems
-        self.first, self.second = first, 1 - first
         self.base = place.z_count - 1
 
     def z_copy(self, shift, z):
         p = self.p
         return remote(self.shard, self.whole.at[p.dp, z, p.c], self.sems, shift - 1, p.along_z(shift))
 
-    def dp_copy(self, slot, owner, bit):
-        p = self.p
-        block = self.whole.at[owner, :, p.c]
-        return remote(block, block, self.sems, self.base + slot, p.along_dp(bit))
-
-    def sent(self):
-        p = self.p
-        return [
-            self.dp_copy(0, p.dp, self.first),
-            self.dp_copy(1, p.dp, self.second),
-            self.dp_copy(2, p.dp_flip(self.first), self.second),
-        ]
-
-    def taken(self):
-        p = self.p
-        return [
-            self.dp_copy(0, p.dp_flip(self.first), self.first),
-            self.dp_copy(1, p.dp_flip(self.second), self.second),
-            self.dp_copy(2, p.dp_flip(2), self.second),
-        ]
+    def own_copy(self, bit, owner):
+        block = self.whole.at[owner, :, self.p.c]
+        return remote(block, block, self.sems, self.base + bit, self.p.along_dp(bit))
+
+    def far_copy(self, bit, lanes, owner):
+        block = self.whole.at[owner, :, self.p.c, :, lanes]
+        return remote(block, block, self.sems, self.base + 2 + bit, self.p.along_dp(1 - bit))
 
     def core_copy(self, core):
         half = self.whole.at[:, :, core]
-        return remote(half, half, self.sems, self.base + 3, self.p.near)
+        return remote(half, half, self.sems, self.base + 4, self.p.near)
 
     def start_z(self):
         p = self.p
@@ -355,19 +422,21 @@
         p = self.p
         for shift in range(1, p.z_count):
             self.z_copy(shift, p.z_at(-shift)).wait_recv()
-        sent = self.sent()
-        sent[0].start()
-        sent[1].start()
+        for bit in range(2):
+            self.own_copy(bit, p.dp).start()
 
     def pass_on(self):
-        self.taken()[0].wait_recv()
-        self.sent()[2].start()
+        p = self.p
+        for bit in range(2):
+            self.own_copy(bit, p.dp_flip(bit)).wait_recv()
+        for bit, lanes in halves(self.whole):
+            self.far_copy(bit, lanes, p.dp_flip(bit)).start()
 
     def start_core(self):
-        taken = self.taken()
-        taken[1].wait_recv()
-        taken[2].wait_recv()
-        self.core_copy(self.p.c).start()
+        p = self.p
+        for bit, lanes in halves(self.whole):
+            self.far_copy(bit, lanes, p.dp_flip(2)).wait_recv()
+        self.core_copy(p.c).start()
 
     def finish(self):
         self.core_copy(1 - self.p.c).wait_recv()
@@ -376,29 +445,29 @@
         p = self.p
         for shift in range(1, p.z_count):
             self.z_copy(shift, p.z).wait_send()
-        for copy in self.sent():
-            copy.wait_send()
+        for bit in range(2):
+            self.own_copy(bit, p.dp).wait_send()
+        for bit, lanes in halves(self.whole):
+            self.far_copy(bit, lanes, p.dp_flip(bit)).wait_send()
         self.core_copy(p.c).wait_send()
 
 
 class Scatter:
-    def __init__(self, place, total, result, bufs, sems, first):
+    def __init__(self, place, total, result, bufs, sems):
         self.p, self.total, self.result, self.sems = place, total, result, sems
         self.out, self.from_core, self.from_dp, self.from_z = bufs
-        self.first, self.second = first, 1 - first
         self.base = place.z_count - 1
 
     def core_copy(self):
-        return remote(self.out, self.from_core, self.sems, self.base + 3, self.p.near)
-
-    def dp_copies(self):
-        p = self.p
-        mine, other, far = (p.dp_flip(bit) for bit in (self.first, self.second, 2))
-        return [
-            remote(self.out.at[far], self.from_dp.at[0], self.sems, self.base, p.along_dp(self.first)),
-            remote(self.out.at[mine], self.from_dp.at[1], self.sems, self.base + 1, p.along_dp(self.first)),
-            remote(self.out.at[other], self.from_dp.at[2], self.sems, self.base + 2, p.along_dp(self.second)),
-        ]
+        return remote(self.out, self.from_core, self.sems, self.base + 6, self.p.near)
+
+    def dp_copy(self, slot, bit, lanes):
+        p = self.p
+        block = p.dp_flip((2, bit, 1 - bit)[slot])
+        return remote(
+            self.out.at[block, :, :, lanes], self.from_dp.at[slot, :, :, lanes], self.sems,
+            self.base + 2 * slot + bit, p.along_dp((bit, bit, 1 - bit)[slot]),
+        )
 
     def z_copy(self, shift):
         p = self.p
@@ -414,64 +483,77 @@
 
         lax.fori_loop(0, p.dp_count * p.z_count, step, 0)
 
+    def rows_at(self, d, z, core):
+        size = self.result.shape[0]
+        start = ((d * self.p.z_count + z) * 2 + core) * size
+        return self.total.at[pl.ds(pl.multiple_of(start, size), size)]
+
+    def mine(self, d, z):
+        if len(self.total.shape) == 4:
+            return self.total.at[d, z]
+        return self.rows_at(d, z, self.p.c)
+
     def start_core(self):
         far = 1 - self.p.c
 
         def body(d, z):
-            self.out[d, z] = self.total[d, z, far].astype(BF)
-
-        self.blocks(body)
+            self.out[d, z] = self.rows_at(d, z, far)[...].astype(BF)
+
+        if len(self.total.shape) == 2:
+            self.blocks(body)
         self.core_copy().start()
 
     def start_dp(self):
-        c = self.p.c
         copy = self.core_copy()
         copy.wait_recv()
         copy.wait_send()
 
         def body(d, z):
-            both = self.total[d, z, c] + self.from_core[d, z].astype(F32)
-            self.total[d, z, c] = both
+            mine = self.mine(d, z)
+            both = mine[...] + self.from_core[d, z].astype(F32)
+            mine[...] = both
             self.out[d, z] = both.astype(BF)
 
         self.blocks(body)
-        copies = self.dp_copies()
-        copies[0].start()
-        copies[1].start()
+        for slot in range(2):
+            for bit, lanes in halves(self.out):
+                self.dp_copy(slot, bit, lanes).start()
 
     def pass_on(self):
         p = self.p
-        copies = self.dp_copies()
-        copies[0].wait_recv()
-        other = p.dp_flip(self.second)
+        for bit, lanes in halves(self.out):
+            self.dp_copy(0, bit, lanes).wait_recv()
+            other = p.dp_flip(1 - bit)
+            for z in range(p.z_count):
+                added = self.mine(other, z)[:, lanes] + self.from_dp[0, z, :, lanes].astype(F32)
+                self.out[other, z, :, lanes] = added.astype(BF)
+            self.dp_copy(2, bit, lanes).start()
+
+    def start_z(self):
+        p = self.p
+        for slot in (1, 2):
+            for bit, lanes in halves(self.out):
+                self.dp_copy(slot, bit, lanes).wait_recv()
         for z in range(p.z_count):
-            added = self.total[other, z, p.c] + self.from_dp[0, z].astype(F32)
-            self.out[other, z] = added.astype(BF)
-        copies[2].start()
-
-    def start_z(self):
-        p = self.p
-        copies = self.dp_copies()
-        copies[1].wait_recv()
-        copies[2].wait_recv()
-        for z in range(p.z_count):
-            added = self.total[p.dp, z, p.c] + self.from_dp[1, z].astype(F32) + self.from_dp[2, z].astype(F32)
-            self.total[p.dp, z, p.c] = added
+            mine = self.mine(p.dp, z)
+            added = mine[...] + self.from_dp[1, z].astype(F32) + self.from_dp[2, z].astype(F32)
+            mine[...] = added
             self.out[p.dp, z] = added.astype(BF)
         for shift in range(1, p.z_count):
             self.z_copy(shift).start()
 
     def finish(self):
         p = self.p
-        added = self.total[p.dp, p.z, p.c]
+        added = self.mine(p.dp, p.z)[...]
         for shift in range(1, p.z_count):
             self.z_copy(shift).wait_recv()
             added = added + self.from_z[shift - 1].astype(F32)
         self.result[...] = added
 
     def drain(self):
-        for copy in self.dp_copies():
-            copy.wait_send()
+        for slot in range(3):
+            for bit, lanes in halves(self.out):
+                self.dp_copy(slot, bit, lanes).wait_send()
         for shift in range(1, self.p.z_count):
             self.z_copy(shift).wait_send()
 
@@ -531,19 +613,15 @@
 
 
 WEIGHTS = ("wk", "wq", "wv", "wm", "we", "ws")
-GRADS = ("gws", "gwe", "gwm", "gwq", "gwk", "gwv")
+GRADS = ("gws", "gwe", "gwm", "gqkv0", "gqkv1")
 EARLY = ("post", "small", "wk", "wq", "wv")
 LATE = ("wm", "we", "ws")
-FIRST = dict(post=0, small=0, wk=1, wq=0, wv=1, wm=0, we=0, ws=1, gws=1, gwe=0, gwm=0, gwq=0, gwk=1, gwv=1, gpost=0)
 
 
 def work_scratch(count, seq, width, ff):
     vm = pltpu.VMEM
     return dict(
-        low=vm((count, seq, width), BF),
-        q=vm((count, seq, width), BF),
-        k=vm((count, seq, width), BF),
-        v=vm((count, seq, width), BF),
+        ab=vm((4, count, seq, width), BF),
         mixed=vm((count, seq, width), BF),
         dfirst=vm((count, seq, width), F32),
         logt=vm((count, HEADS, seq), F32),
@@ -552,27 +630,21 @@
         ot=vm((width, seq), BF),
         mask=vm((seq, seq), F32),
         xh1=vm((seq // FF_PARTS, width), F32),
-        nl=vm((seq, width), BF),
-        gff=vm((seq, width), BF),
-        act=vm((seq // FF_PARTS, ff), BF),
+        nl=vm((count, seq, width), BF),
+        gff=vm((count, seq, width), BF),
         slope=vm((seq // FF_PARTS, ff), F32),
         gpos=vm((seq, width), F32),
         x=vm((count, seq, width), BF),
         go=vm((count, seq, width), BF),
         io_sem=pltpu.SemaphoreType.DMA((4, count)),
+        part_sem=pltpu.SemaphoreType.DMA((2, 2, 4)),
+        park_sem=pltpu.SemaphoreType.DMA((4, count)),
+        load_sem=pltpu.SemaphoreType.DMA((4,)),
     )
 
 
 def zero_sums(r):
-    for name in GRADS:
-        ref = getattr(r, name)
-
-        def step(at, carry):
-            ref[at // ref.shape[1], lax.rem(at, ref.shape[1])] = jnp.zeros(ref.shape[2:], ref.dtype)
-            return carry
-
-        lax.fori_loop(0, ref.shape[0] * ref.shape[1], step, 0)
-    for name in ("gpos", "gvec", "geb"):
+    for name in ("gwm", "gpos", "gvec", "geb"):
         ref = getattr(r, name)
         ref[...] = jnp.zeros(ref.shape, ref.dtype)
 
@@ -591,6 +663,33 @@
         return pltpu.make_async_copy(r.x.at[w], r.gin.at[w], r.io_sem.at[3, w])
 
     return load, store_out, store_gin
+
+
+def emit_whole(r, item, value):
+    size = value.shape[0]
+    if item < r.ws.shape[0]:
+        r.gws[item * size : (item + 1) * size, :] = value
+    else:
+        c = item - r.ws.shape[0]
+        r.gwe[:, c * size : (c + 1) * size] = value
+
+
+def emit_halves(r, place, item, value):
+    r.mask[...] = value
+    chunks, size = r.ws.shape[0], value.shape[0]
+    if item < chunks:
+        blocks = [((item, z), z) for z in range(place.z_count)]
+        kept, sent, rows = r.gws, r.gws_out, r.gws.shape[2]
+        cols = slice(None)
+    else:
+        blocks = [((d, z), d * place.z_count + z) for d in range(place.dp_count) for z in range(place.z_count)]
+        kept, sent, rows = r.gwe, r.gwe_out, r.gwe.shape[2]
+        cols = slice((item - chunks) * size, (item - chunks + 1) * size)
+    for at, block in blocks:
+        start = pl.multiple_of((block * 2 + place.c) * rows, rows)
+        kept[at + (slice(None), cols)] = r.mask[pl.ds(start, rows), :]
+        start = pl.multiple_of((block * 2 + 1 - place.c) * rows, rows)
+        sent[at + (slice(None), cols)] = r.mask[pl.ds(start, rows), :].astype(BF)
 
 
 def alone_kernel(names, *refs):
@@ -606,16 +705,21 @@
             copy.wait()
 
     def second(w):
-        windows(FF_PARTS, lambda part: feed_forward(w, part, r))
+        feed_forward(w, 0, r)
         store_out(w).start()
 
     def third(w):
-        attention_backward(w, r, lambda w: None)
+        hidden_back(w, r)
         store_gin(w).start()
 
     windows(count, lambda w: hidden_and_keys(w, r))
-    windows(count, lambda w: attention_forward(w, r, lambda w: None))
+    windows(count, lambda w: attention_forward(w, r))
+    finish_parking(r)
     windows(count, second)
+    weight_sums(r, lambda item, value: emit_whole(r, item, value), lambda item: None)
+    for group in range(GROUPS):
+        windows(count, lambda w: attention_backward(w, group, r))
+        projection_sums(group, r)
     windows(count, third)
     r.gpos_out[...] = r.gpos[...]
     for w in range(count):
@@ -675,7 +779,7 @@
     for name in EARLY + LATE:
         shard = r.small_low if name == "small" else getattr(r, name + "_shard")
         sems = (getattr(r, name + "_send"), getattr(r, name + "_recv"))
-        gathers[name] = Gather(place, shard, getattr(r, name), sems, FIRST[name])
+        gathers[name] = Gather(place, shard, getattr(r, name), sems)
     early = [gathers[name] for name in EARLY]
     late = [gathers[name] for name in LATE]
     place.barrier()
@@ -703,52 +807,90 @@
 
     wm, we, ws = late
     first_plan = ((1, (wm.pass_on, we.pass_on)), (3, (ws.pass_on, wm.start_core)))
-    first_mid = ()
 
     def first_body(w):
         at_window(w, first_plan)
-        attention_forward(w, r, lambda at: at_window(at, first_mid))
+        attention_forward(w, r)
 
     windows(count, first_body)
     we.start_core()
     ws.start_core()
+    finish_parking(r)
     for job in late:
         job.finish()
 
     def second_body(w):
-        windows(FF_PARTS, lambda part: feed_forward(w, part, r))
+        feed_forward(w, 0, r)
         store_out(w).start()
 
     windows(count, second_body)
 
     scatters = {}
+    for job in early + late:
+        job.drain()
     for name in GRADS + ("gpost",):
-        total = r.gpost_sum if name == "gpost" else getattr(r, name)
-        bufs = [getattr(r, name + tail) for tail in ("_out", "_core", "_dp", "_z")]
+        total = r.mask if name == "gpost" else getattr(r, name)
+        if name.startswith("gqkv"):
+            group, size = int(name[-1]), getattr(r, name).shape[1]
+            out = r.we.at[:, :, 1, :, pl.ds(group * size, size)]
+        else:
+            out = getattr(r, "post" if name == "gpost" else "w" + name[2:]).at[:, :, 0]
+        setattr(r, name + "_out", out)
+        bufs = [out] + [getattr(r, name + tail) for tail in ("_core", "_dp", "_z")]
         sems = (getattr(r, name + "_send"), getattr(r, name + "_recv"))
-        scatters[name] = Scatter(place, total, getattr(r, name + "_result"), bufs, sems, FIRST[name])
+        scatters[name] = Scatter(place, total, getattr(r, name + "_result"), bufs, sems)
     sums = SumAll(
         place, r.gsmall, r.gsmall_result, (r.gsmall_dp, r.gsmall_z, r.gsmall_in), (r.gsmall_send, r.gsmall_recv)
     )
     gws, gwe, gwm = (scatters[name] for name in ("gws", "gwe", "gwm"))
-    last = [scatters[name] for name in ("gwq", "gwk", "gwv", "gpost")]
-    gws.start_core()
-    gwe.start_core()
+    early_qkv, late_qkv, post = (scatters[name] for name in ("gqkv0", "gqkv1", "gpost"))
     gwm.start_core()
-    third_plan = ((1, (gwe.start_dp, gwm.start_dp)), (3, (gwe.pass_on, gwm.pass_on)))
-    third_mid = ((0, (gws.start_dp,)), (2, (gws.pass_on,)), (3, (gws.start_z,)))
-
-    def third_body(w):
-        at_window(w, third_plan)
-        attention_backward(w, r, lambda at: at_window(at, third_mid))
+
+    def after(item):
+        if item == 1:
+            gwm.start_dp()
+        if item == 3:
+            gws.start_core()
+            gwm.pass_on()
+        if item == 5:
+            gwm.start_z()
+        if item == 6:
+            gws.start_dp()
+        if item == 7:
+            gwe.start_core()
+
+    weight_sums(r, lambda item, value: emit_halves(r, place, item, value), after)
+
+    plans = (
+        ((1, (gws.pass_on,)), (2, (gwe.start_dp,)), (3, (gws.start_z,))),
+        ((1, (early_qkv.start_dp,)), (2, (gwe.start_z,)), (3, (early_qkv.pass_on,))),
+        ((2, (late_qkv.start_dp,)),),
+    )
+
+    def heads_body(group):
+        def body(w):
+            at_window(w, plans[group])
+            attention_backward(w, group, r)
+
+        return body
+
+    windows(count, heads_body(0))
+    projection_sums(0, r)
+    early_qkv.start_core()
+    gwe.pass_on()
+    windows(count, heads_body(1))
+    projection_sums(1, r)
+    late_qkv.start_core()
+    early_qkv.start_z()
+
+    def last_body(w):
+        at_window(w, plans[2])
+        hidden_back(w, r)
         store_gin(w).start()
 
-    windows(count, third_body)
-    for job in last[:3]:
-        job.start_core()
-    add_blocks = r.gpos[...].T
-    r.gpost_sum[...] = add_blocks.reshape(r.gpost_sum.shape)
-    last[3].start_core()
+    windows(count, last_body)
+    r.mask[...] = r.gpos[...].T
+    post.start_core()
     ff_rows = r.geb.shape[1] // r.gvec.shape[1]
     width = r.gvec.shape[1]
     r.gsmall[0:8, :] = r.gvec[...]
@@ -756,19 +898,17 @@
     for i in range(ff_rows):
         r.gsmall[8 + i : 9 + i, :] = r.geb[:, i * width : (i + 1) * width]
     sums.start_core()
-    last = last + [sums]
-    for job in last:
-        job.start_dp()
-    gwe.start_z()
-    gwm.start_z()
-    for job in last:
-        job.pass_on()
-    for job in last:
-        job.start_z()
-    everyone = [gws, gwe, gwm] + last
+    late_qkv.pass_on()
+    post.start_dp()
+    sums.start_dp()
+    post.pass_on()
+    late_qkv.start_z()
+    sums.start_z()
+    post.start_z()
+    everyone = [gws, gwe, gwm, early_qkv, late_qkv, sums, post]
     for job in everyone:
         job.finish()
-    for job in early + late + everyone:
+    for job in everyone:
         job.drain()
     for w in range(count):
         store_out(w).wait()
@@ -789,8 +929,13 @@
     for load, store in zip(loads, stores):
         load.wait()
         store.start()
-    for name in GRADS:
+    for name in GRADS[:3]:
         getattr(r, name)[...] = getattr(r, name + "_in")[...]
+    size = r.gwq.shape[1] // GROUPS
+    for group in range(GROUPS):
+        source = getattr(r, "gqkv" + str(group) + "_in")
+        for at, name in enumerate(("gwq", "gwk", "gwv")):
+            getattr(r, name)[:, group * size : (group + 1) * size] = source[:, at * size : (at + 1) * size]
     r.gpos[...] = r.gpost_in[...].T
     place = Place(*counts)
     me = (place.dp * place.z_count + place.z) * 2 + place.c
@@ -835,6 +980,7 @@
     shape_of = jax.ShapeDtypeStruct
     merged = lambda a: a.reshape((count,) + a.shape[2:])
     act = shape_of((count, seq, width), BF)
+    kept = shape_of((3, 4, count, seq, width), BF)
     data = dict(
         lens=(lengths, pltpu.SMEM), x_in=(merged(inputs), hbm), go_in=(merged(grad_out), hbm)
     )
@@ -849,8 +995,9 @@
         for i, vector in enumerate(vectors):
             ins["vec" + str(i)] = (vector[None], vm)
         ins["ebs"] = (eb[None], vm)
-        outs = dict(out=(act, hbm), gin=(act, hbm))
-        results = dict(gwq=wq, gwk=wk, gwv=wv, gwm=wm, gwe=we, gws=ws, gpost=pos.T)
+        outs = dict(out=(act, hbm), gin=(act, hbm), kept=(kept, hbm))
+        part = shape_of((rows, 3 * width // GROUPS), F32)
+        results = dict(gqkv0=part, gqkv1=part, gwm=wm, gwe=we, gws=ws, gpost=pos.T)
         for name, like in results.items():
             outs[name + "_result"] = (shape_of(like.shape, F32), vm)
         outs["gsmall_result"] = (shape_of((16, width), F32), vm)
@@ -870,8 +1017,10 @@
         scratch.update(pair("small"))
         scratch.update(pair("gsmall"))
         for name, like in results.items():
-            scratch["gpost_sum" if name == "gpost" else name] = vm(lead + like.shape, F32)
-            scratch[name + "_out"] = vm(lead[:2] + like.shape, BF)
+            if name in ("gws", "gwe"):
+                scratch[name] = vm(lead[:2] + like.shape, F32)
+            elif name != "gpost":
+                scratch[name] = vm((like.shape[0] * dp_count * fsdp_count, like.shape[1]), F32)
             scratch[name + "_core"] = vm(lead[:2] + like.shape, BF)
             scratch[name + "_dp"] = vm((3,) + lead[1:2] + like.shape, BF)
             scratch[name + "_z"] = vm((lead[1] - 1,) + like.shape, BF)
@@ -889,8 +1038,8 @@
         for name in GRADS + ("gpost", "gsmall"):
             ins[name + "_in"] = (got[name + "_result"], vm)
         outs = dict(out=(act, hbm), gin=(act, hbm))
-        for name in GRADS:
-            outs[name] = (shape_of(results[name].shape, F32), vm)
+        for name, like in dict(gwq=wq, gwk=wk, gwv=wv, gwm=wm, gwe=we, gws=ws).items():
+            outs[name] = (shape_of(like.shape, F32), vm)
         outs["gpos"] = (shape_of(pos.shape, F32), vm)
         outs["gvec"] = (shape_of((8, rows), F32), vm)
         outs["geb"] = (shape_of((1, ff_rows), F32), vm)
@@ -911,14 +1060,20 @@
         ins["pos"] = (gather(pos, 1), vm)
         ins["vec"] = (jnp.stack([gather(a).astype(F32) for a in vectors]), vm)
         ins["eb"] = (gather(eb).astype(F32)[None], vm)
-        outs = dict(out=(act, hbm), gin=(act, hbm))
-        for name in GRADS:
-            outs[name] = (shape_of(ins["w" + name[2:]][0].shape, F32), vm)
+        outs = dict(out=(act, hbm), gin=(act, hbm), kept=(kept, hbm))
+        for name, shape in dict(gws=(ff, width), gwe=(width, ff), gwm=(width, width)).items():
+            outs[name] = (shape_of(shape, F32), vm)
+        for group in range(GROUPS):
+            outs["gqkv" + str(group)] = (shape_of((width, 3 * width // GROUPS), F32), vm)
         outs["gpos_out"] = (shape_of((seq, width), F32), vm)
         outs["gvec"] = (shape_of((8, width), F32), vm)
         outs["geb"] = (shape_of((1, ff), F32), vm)
         got = call(alone_kernel, "layer_alone", ins, outs, scratch)
-        grads = {name: share(flat(got[name])) for name in GRADS}
+        size = width // GROUPS
+        for at, name in enumerate(("gwq", "gwk", "gwv")):
+            parts = [got["gqkv" + str(g)][:, at * size : (at + 1) * size] for g in range(GROUPS)]
+            got[name] = jnp.concatenate(parts, axis=1)
+        grads = {name: share(got[name]) for name in ("gwq", "gwk", "gwv", "gwm", "gwe", "gws")}
         gpos = share(got["gpos_out"], 1)
         gvec = [share(got["gvec"][i]) for i in range(8)]
         geb = share(got["geb"][0])

time: 168 us -> 156 us (0.929)
  Pallas kernels: 163 us -> 152 us
    pallas_call x2, Pallas kernels: 163 us -> 152 us  [call(): pl.pallas_call(functools.partial(kernel, names), out_shape=tuple((shape f...]
where the time goes in v4:
time: 156 us
  Pallas kernels  152 us (97%)
  local copies, waits for them, and re-layouts  3.19 us (2%)
    pallas_call x2, Pallas kernels, call(): pl.pallas_call(functools.partial(kernel, names), out_shape=tuple((shape f...  152 us

profile of v4, /device:TPU:0, one launch (start us, length us, event | category | flops | bytes accessed | tf_op | source)
XLA Modules:
  0.0 156.0 jit_solution(9237710100193746720)
XLA Ops:
  0.7 146.6 %layer.1 = (bf16[4,512,512]{2,1,0:T(8,128)(2,1)}, bf16[4,512,512]{2,1,0:T(8,128)(2,1)}, bf16[3,4,4,512,512]{4,3,2,1,0:T(8,128)(2,1)}, f32[16,768]{1,0:T(8,128)},...) custom-call(s32[2,2]{1,0:T(2,128)} %refs_0_.1, ...), custom_call_target="tpu_custom_call" | custom-call | tf_op jit(solution)/shard_map/layer/pallas_call | solution.py:959
  147.3 5.5 %unpack.1 = (bf16[4,512,512]{2,1,0:T(8,128)(2,1)}, bf16[4,512,512]{2,1,0:T(8,128)(2,1)}, f32[16,512]{1,0:T(8,128)}, f32[16,512]{1,0:T(8,128)}, f32[16,512]{1,0:T...) custom-call(bf16[4,512,512]{2,1,0:T(8,128)(2,1)} %get-tuple-element., ...), custom_call_target="tpu_custom_call" | custom-call | tf_op jit(solution)/shard_map/unpack/pallas_call | solution.py:959
  152.8 1.5 slice_bitcast_fusion
  154.3 1.7 %copy.37 = f32[512,16]{0,1:T(8,128)} copy(f32[512,16]{1,0:T(8,128)} %get-tuple-element.66) | data formatting | bytes 65536

commit v5 on v4

--- a/solution.py
+++ b/solution.py
@@ -63,6 +63,13 @@
     query_at = lax.broadcasted_iota(jnp.int32, (seq, seq), 1)
     ok = (key_at <= query_at) & (key_at < length_of(w, r))
     r.mask[...] = jnp.where(ok, 0.0, -1e30)
+
+
+def make_causal(r):
+    size = r.causal.shape[0]
+    key_at = lax.broadcasted_iota(jnp.int32, (size, size), 0)
+    query_at = lax.broadcasted_iota(jnp.int32, (size, size), 1)
+    r.causal[...] = jnp.where(key_at <= query_at, 0.0, -1e30)
 
 
 def hidden_and_keys(w, r):
@@ -100,7 +107,8 @@
         n_all = jnp.sum(e0, axis=0, keepdims=True)
         n_right = n_all[:, half:] + jnp.sum(e1, axis=0, keepdims=True)
         total = jnp.concatenate([n_all[:, :half], n_right], axis=1)
-        r.logt[w, h : h + 1, :] = top + jnp.log(total)
+        query_at = lax.broadcasted_iota(jnp.int32, (1, seq), 1)
+        r.logt[w, h : h + 1, :] = jnp.where(query_at < length_of(w, r), top + jnp.log(total), 1e30)
         inv = 1.0 / total
         p0 = (e0 * inv).astype(BF)
         p1 = (e1 * inv[:, half:]).astype(BF)
@@ -260,7 +268,6 @@
     head = width // HEADS
     scale = head**-0.5
     cols = slice(group * (width // GROUPS), (group + 1) * (width // GROUPS))
-    make_mask(w, r)
     r.vt[cols, :] = r.ab[K, w, :, cols].T
     lane = lax.broadcasted_iota(jnp.int32, (seq, 2 * head), 1)
     pairs = HEADS // 2 // GROUPS
@@ -276,8 +283,10 @@
             gh = jnp.where(mine, r.mixed[w, :, pair], jnp.zeros((), BF))
             logt = r.logt[w, h : h + 1, :]
             delta = r.delta[w, h : h + 1, :]
-            p0 = jnp.exp(nt(kp[:half], qh) + r.mask[:half, :] - logt)
-            p1 = jnp.exp(nt(kp[half:], qh[half:]) + r.mask[half:, half:] - logt[:, half:])
+            s0 = nt(kp[:half], qh)
+            s0 = jnp.concatenate([s0[:, :half] + r.causal[...], s0[:, half:]], axis=1)
+            p0 = jnp.exp(s0 - logt)
+            p1 = jnp.exp(nt(kp[half:], qh[half:]) + r.causal[...] - logt[:, half:])
             d0 = (p0 * (nt(vp[:half], gh) - delta)).astype(BF)
             d1 = (p1 * (nt(vp[half:], gh[half:]) - delta[:, half:])).astype(BF)
             p0 = p0.astype(BF)
@@ -381,7 +390,7 @@
 
 
 def hop_count(dp_count, z_count):
-    return (z_count - 1) + 7
+    return (z_count - 1) + 10
 
 
 def halves(ref):
@@ -458,8 +467,11 @@
         self.out, self.from_core, self.from_dp, self.from_z = bufs
         self.base = place.z_count - 1
 
-    def core_copy(self):
-        return remote(self.out, self.from_core, self.sems, self.base + 6, self.p.near)
+    pieces = ((slice(None), slice(None)),)
+
+    def core_copy(self, piece):
+        at = self.pieces[piece]
+        return remote(self.out.at[at], self.from_core.at[at], self.sems, self.base + 6 + piece, self.p.near)
 
     def dp_copy(self, slot, bit, lanes):
         p = self.p
@@ -499,14 +511,13 @@
         def body(d, z):
             self.out[d, z] = self.rows_at(d, z, far)[...].astype(BF)
 
-        if len(self.total.shape) == 2:
-            self.blocks(body)
-        self.core_copy().start()
+        self.blocks(body)
+        self.core_copy(0).start()
 
     def start_dp(self):
-        copy = self.core_copy()
-        copy.wait_recv()
-        copy.wait_send()
+        for piece in range(len(self.pieces)):
+            self.core_copy(piece).wait_recv()
+            self.core_copy(piece).wait_send()
 
         def body(d, z):
             mine = self.mine(d, z)
@@ -629,6 +640,7 @@
         vt=vm((width, seq), BF),
         ot=vm((width, seq), BF),
         mask=vm((seq, seq), F32),
+        causal=vm((seq // 2, seq // 2), F32),
         xh1=vm((seq // FF_PARTS, width), F32),
         nl=vm((count, seq, width), BF),
         gff=vm((count, seq, width), BF),
@@ -644,6 +656,7 @@
 
 
 def zero_sums(r):
+    make_causal(r)
     for name in ("gwm", "gpos", "gvec", "geb"):
         ref = getattr(r, name)
         ref[...] = jnp.zeros(ref.shape, ref.dtype)
@@ -845,19 +858,24 @@
     gws, gwe, gwm = (scatters[name] for name in ("gws", "gwe", "gwm"))
     early_qkv, late_qkv, post = (scatters[name] for name in ("gqkv0", "gqkv1", "gpost"))
     gwm.start_core()
+    chunks = counts[0]
+    gws.pieces = tuple((c, slice(None)) for c in range(chunks))
+    size = r.we.shape[-1] // chunks
+    gwe.pieces = tuple(
+        (slice(None), slice(None), slice(None), slice(c * size, (c + 1) * size)) for c in range(chunks)
+    )
 
     def after(item):
+        job = gws if item < chunks else gwe
+        job.core_copy(item % chunks).start()
         if item == 1:
             gwm.start_dp()
         if item == 3:
-            gws.start_core()
             gwm.pass_on()
         if item == 5:
             gwm.start_z()
         if item == 6:
             gws.start_dp()
-        if item == 7:
-            gwe.start_core()
 
     weight_sums(r, lambda item, value: emit_halves(r, place, item, value), after)
 
@@ -936,13 +954,14 @@
         source = getattr(r, "gqkv" + str(group) + "_in")
         for at, name in enumerate(("gwq", "gwk", "gwv")):
             getattr(r, name)[:, group * size : (group + 1) * size] = source[:, at * size : (at + 1) * size]
-    r.gpos[...] = r.gpost_in[...].T
+    r.gpost[...] = r.gpost_in[...]
     place = Place(*counts)
     me = (place.dp * place.z_count + place.z) * 2 + place.c
-    rows, ff_rows = r.gvec.shape[1], r.geb.shape[1]
+    rows, ff_rows = r.gvec0.shape[1], r.geb.shape[1]
     width = r.gsmall_in.shape[1]
     turned = pltpu.roll(r.gsmall_in[0:8, :], width - me * rows, axis=1)
-    r.gvec[...] = turned[:, :rows]
+    for i in range(8):
+        getattr(r, "gvec" + str(i))[...] = turned[i : i + 1, :rows]
     start = me * ff_rows
     lines = r.gsmall_in[8:16, :]
     line_at = lax.broadcasted_iota(jnp.int32, (8, width), 0)
@@ -1040,14 +1059,16 @@
         outs = dict(out=(act, hbm), gin=(act, hbm))
         for name, like in dict(gwq=wq, gwk=wk, gwv=wv, gwm=wm, gwe=we, gws=ws).items():
             outs[name] = (shape_of(like.shape, F32), vm)
-        outs["gpos"] = (shape_of(pos.shape, F32), vm)
-        outs["gvec"] = (shape_of((8, rows), F32), vm)
+        outs["gpost"] = (shape_of((rows, seq), F32), vm)
+        for i in range(8):
+            outs["gvec" + str(i)] = (shape_of((1, rows), F32), vm)
         outs["geb"] = (shape_of((1, ff_rows), F32), vm)
         got = call(
             functools.partial(unpack_kernel, counts), "unpack", ins, outs,
             dict(held=vm((2,) + act.shape, BF), sem=pltpu.SemaphoreType.DMA((2, 2, count))),
         )
-        gvec, geb, gpos = got["gvec"], got["geb"][0], got["gpos"]
+        gvec = [got["gvec" + str(i)].reshape(rows) for i in range(8)]
+        geb, gpos = got["geb"].reshape(ff_rows), got["gpost"].T
         grads = got
     else:
         lead = (4, 4, 2)

time: 156 us -> 154 us (0.987)
  local copies, waits for them, and re-layouts: 3.19 us -> 0 us
    unnamed x1 -> x0, local copies, waits for them, and re-layouts: 1.67 us -> none
where the time goes in v5:
time: 154 us; the launch traced here: 153 us
  Pallas kernels  153 us (99%)
    pallas_call x2, Pallas kernels, call(): pl.pallas_call(functools.partial(kernel, names), out_shape=tuple((shape f...  153 us

profile of v5, /device:TPU:0, one launch (start us, length us, event | category | flops | bytes accessed | tf_op | source)
XLA Modules:
  0.0 153.5 jit_solution(8508270366991674830)
XLA Ops:
  0.7 147.2 %layer.1 = (bf16[4,512,512]{2,1,0:T(8,128)(2,1)}, bf16[4,512,512]{2,1,0:T(8,128)(2,1)}, bf16[3,4,4,512,512]{4,3,2,1,0:T(8,128)(2,1)}, f32[16,768]{1,0:T(8,128)},...) custom-call(s32[2,2]{1,0:T(2,128)} %refs_0_.1, ...), custom_call_target="tpu_custom_call" | custom-call | tf_op jit(solution)/shard_map/layer/pallas_call | solution.py:978
  147.9 5.4 %unpack.1 = (bf16[4,512,512]{2,1,0:T(8,128)(2,1)}, bf16[4,512,512]{2,1,0:T(8,128)(2,1)}, f32[16,512]{1,0:T(8,128)}, f32[16,512]{1,0:T(8,128)}, f32[16,512]{1,0:T...) custom-call(bf16[4,512,512]{2,1,0:T(8,128)(2,1)} %get-tuple-element., ...), custom_call_target="tpu_custom_call" | custom-call | tf_op jit(solution)/shard_map/unpack/pallas_call | solution.py:978

commit v6 on v5

--- a/solution.py
+++ b/solution.py
@@ -514,20 +514,19 @@
         self.blocks(body)
         self.core_copy(0).start()
 
+    def summed(self, d, z, lanes):
+        return self.mine(d, z)[:, lanes] + self.from_core[d, z, :, lanes].astype(F32)
+
     def start_dp(self):
+        p = self.p
         for piece in range(len(self.pieces)):
             self.core_copy(piece).wait_recv()
             self.core_copy(piece).wait_send()
-
-        def body(d, z):
-            mine = self.mine(d, z)
-            both = mine[...] + self.from_core[d, z].astype(F32)
-            mine[...] = both
-            self.out[d, z] = both.astype(BF)
-
-        self.blocks(body)
         for slot in range(2):
             for bit, lanes in halves(self.out):
+                block = p.dp_flip((2, bit)[slot])
+                for z in range(p.z_count):
+                    self.out[block, z, :, lanes] = self.summed(block, z, lanes).astype(BF)
                 self.dp_copy(slot, bit, lanes).start()
 
     def pass_on(self):
@@ -536,26 +535,27 @@
             self.dp_copy(0, bit, lanes).wait_recv()
             other = p.dp_flip(1 - bit)
             for z in range(p.z_count):
-                added = self.mine(other, z)[:, lanes] + self.from_dp[0, z, :, lanes].astype(F32)
+                added = self.summed(other, z, lanes) + self.from_dp[0, z, :, lanes].astype(F32)
                 self.out[other, z, :, lanes] = added.astype(BF)
             self.dp_copy(2, bit, lanes).start()
+
+    def along(self, z):
+        added = self.summed(self.p.dp, z, slice(None))
+        return added + self.from_dp[1, z].astype(F32) + self.from_dp[2, z].astype(F32)
 
     def start_z(self):
         p = self.p
         for slot in (1, 2):
             for bit, lanes in halves(self.out):
                 self.dp_copy(slot, bit, lanes).wait_recv()
-        for z in range(p.z_count):
-            mine = self.mine(p.dp, z)
-            added = mine[...] + self.from_dp[1, z].astype(F32) + self.from_dp[2, z].astype(F32)
-            mine[...] = added
-            self.out[p.dp, z] = added.astype(BF)
         for shift in range(1, p.z_count):
+            z = p.z_at(shift)
+            self.out[p.dp, z] = self.along(z).astype(BF)
             self.z_copy(shift).start()
 
     def finish(self):
         p = self.p
-        added = self.mine(p.dp, p.z)[...]
+        added = self.along(p.z)
         for shift in range(1, p.z_count):
             self.z_copy(shift).wait_recv()
             added = added + self.from_z[shift - 1].astype(F32)
@@ -819,14 +819,13 @@
         job.finish()
 
     wm, we, ws = late
-    first_plan = ((1, (wm.pass_on, we.pass_on)), (3, (ws.pass_on, wm.start_core)))
+    first_plan = ((1, (wm.pass_on,)), (2, (we.pass_on, wm.start_core)), (3, (ws.pass_on, we.start_core)))
 
     def first_body(w):
         at_window(w, first_plan)
         attention_forward(w, r)
 
     windows(count, first_body)
-    we.start_core()
     ws.start_core()
     finish_parking(r)
     for job in late:

time: 154 us -> 151 us (0.981)
  Pallas kernels: 153 us -> 150 us
    pallas_call x2, Pallas kernels: 153 us -> 150 us  [call(): pl.pallas_call(functools.partial(kernel, names), out_shape=tuple((shape f...]
where the time goes in v6:
time: 151 us
  Pallas kernels  150 us (99%)
    pallas_call x2, Pallas kernels, call(): pl.pallas_call(functools.partial(kernel, names), out_shape=tuple((shape f...  150 us

profile of v6, /device:TPU:0, one launch (start us, length us, event | category | flops | bytes accessed | tf_op | source)
XLA Modules:
  0.0 150.7 jit_solution(1951257593423888394)
XLA Ops:
  0.7 144.5 %layer.1 = (bf16[4,512,512]{2,1,0:T(8,128)(2,1)}, bf16[4,512,512]{2,1,0:T(8,128)(2,1)}, bf16[3,4,4,512,512]{4,3,2,1,0:T(8,128)(2,1)}, f32[16,768]{1,0:T(8,128)},...) custom-call(s32[2,2]{1,0:T(2,128)} %refs_0_.1, ...), custom_call_target="tpu_custom_call" | custom-call | tf_op jit(solution)/shard_map/layer/pallas_call | solution.py:977
  145.2 5.4 %unpack.1 = (bf16[4,512,512]{2,1,0:T(8,128)(2,1)}, bf16[4,512,512]{2,1,0:T(8,128)(2,1)}, f32[16,512]{1,0:T(8,128)}, f32[16,512]{1,0:T(8,128)}, f32[16,512]{1,0:T...) custom-call(bf16[4,512,512]{2,1,0:T(8,128)(2,1)} %get-tuple-element., ...), custom_call_target="tpu_custom_call" | custom-call | tf_op jit(solution)/shard_map/unpack/pallas_call | solution.py:977
